TPU v7x, 256 devices: a whole 4x4x8 slice. The times are simulated.
256 devices in a mesh: inline: 8 (over z_hi, core), tile: 32 (over z_lo, y, x).
Axes of the slice: x: 4, y: 4, z: 8 (z_hi: 4, z_lo: 2; z = z_hi * 2 + z_lo), core: 2. Of those that a mesh axis runs over, the one named last changes fastest.
Arguments:
- features: bfloat16 [96, 16, 64, 128], P(None, 'inline', 'tile'), may hold values from -13 to 13
- conv1_weight: bfloat16 [96, 27, 96], replicated, may hold values from -0.125 to 0.125
- conv2_weight: bfloat16 [96, 27, 96], replicated, may hold values from -0.125 to 0.125
- fault_head: bfloat16 [96, 2], replicated, may hold values from -0.625 to 0.625
- horizon_head: bfloat16 [96, 4], replicated, may hold values from -0.625 to 0.625
- salt_query: bfloat16 [96], replicated, may hold values from -0.625 to 0.625
- salt_head: bfloat16 [96, 2], replicated, may hold values from -0.625 to 0.625
- fault_labels: int32 [16, 64, 128], P('inline', 'tile'), may hold values from 0 to 1
- horizon_labels: int32 [16, 64, 128], P('inline', 'tile'), may hold values from 0 to 3
- salt_labels: int32 [16, 128], P('inline'), may hold values from 0 to 1
Outputs:
- grads: float32 [2, 3, 248832], P(None, None, ('inline', 'tile'))
- gram: float32 [2, 3, 3], replicated
All inputs are finite; a program needn't handle non-finite values.
Results may differ from a plain program's by a relative error of at most 0.0043.
Values may be sent and summed in bfloat16 or wider, within the bound.
A program may use at most 128 MiB of HBM per device.

v0:
```python
import functools
import math

import jax
import jax.numpy as jnp
from jax import lax
from jax.sharding import Mesh
from jax.sharding import PartitionSpec as P

D1 = 1
D2 = 2
TILE = ("tile_0", "tile_1", "tile_2")
INLINE = ("inline_0", "inline_1")
INLINE_TILE = ("inline_0", "inline_1", "tile_0", "tile_1", "tile_2")


CAPPING = 8.0
HIGH = lax.Precision.HIGHEST


def padded_2(x, sides, width):
    for axis, dim in sides:
        count, length = (lax.axis_size(axis), x.shape[dim])
        up = [(i, (i + 1) % count) for i in range(count - 1)]
        down = [(j, i) for i, j in up]
        last = lax.slice_in_dim(x, length - width, length, axis=dim)
        initial = lax.slice_in_dim(x, 0, width, axis=dim)
        before = lax.ppermute(last, axis, up)
        after = lax.ppermute(initial, axis, down)
        x = jnp.concatenate([before, x, after], axis=dim)
    return x


def by_axis(x, axes):
    return functools.reduce(lax.psum, axes, x)


def capped(value):
    return CAPPING * jnp.tanh(value / CAPPING)


def cap_slope(value):
    squash = jnp.tanh(value / CAPPING)
    return 1.0 - squash * squash


def silu_slope(value):
    sig = jax.nn.sigmoid(value)
    return sig * (1.0 + value * (1.0 - sig))


def pad_cross(field, dilation):
    return jnp.pad(field, [(0, 0)] * (field.ndim - 1) + [(dilation, dilation)])


def conv_local(padded, weight, dilation, inline_cells, depth_cells, cross_cells):
    result = None
    for along_x in range(3):
        for along_z in range(3):
            block = padded[
                :,
                :,
                along_x * dilation : along_x * dilation + inline_cells,
                along_z * dilation : along_z * dilation + depth_cells,
                :,
            ]
            taps = jnp.stack(
                [
                    block[..., along_y * dilation : along_y * dilation + cross_cells]
                    for along_y in range(3)
                ],
                axis=2,
            )
            first_tap = (along_x * 3 + along_z) * 3
            kernel = weight[:, first_tap : first_tap + 3, :]
            term = jnp.einsum("ikd,bikxzy->bdxzy", kernel, taps, preferred_element_type=jnp.float32)
            result = term if result is None else result + term
    return result


def weight_local(padded, deltas, dilation, inline_cells, depth_cells, cross_cells):
    pieces = []
    for along_x in range(3):
        for along_z in range(3):
            block = padded[
                :,
                along_x * dilation : along_x * dilation + inline_cells,
                along_z * dilation : along_z * dilation + depth_cells,
                :,
            ]
            taps = jnp.stack(
                [
                    block[..., along_y * dilation : along_y * dilation + cross_cells]
                    for along_y in range(3)
                ],
                axis=1,
            )
            pieces.append(
                jnp.einsum("ikxzy,toxzy->tiko", taps, deltas, preferred_element_type=jnp.float32)
            )
    return jnp.concatenate(pieces, axis=2)


def head_cotangent(second_out, head, labels, scale):
    raw = jnp.einsum("cxzy,cn->nxzy", second_out, head, preferred_element_type=jnp.float32)
    expo = jnp.exp(capped(raw))
    prob = expo / jnp.sum(expo, axis=0, keepdims=True)
    classes = jnp.arange(head.shape[1], dtype=jnp.int32)
    onehot = (labels[None] == classes[:, None, None, None]).astype(jnp.float32)
    dlog = (prob - onehot) * cap_slope(raw) * scale
    return jnp.einsum("cn,nxzy->cxzy", head.astype(jnp.float32), dlog, precision=HIGH)


def trace_stats(field, query):
    raw = jnp.einsum("cxzy,c->xzy", field, query, preferred_element_type=jnp.float32)
    expo = jnp.exp(capped(raw))
    total = jnp.sum(expo, axis=1)
    num = jnp.einsum("xzy,cxzy->cxy", expo, field.astype(jnp.float32), precision=HIGH)
    return (raw, expo, num, total)


def trace_backward(field32, raw, expo, num, total, query, head, labels, scale):
    head32 = head.astype(jnp.float32)
    pooled = num / total[None]
    salt_raw = jnp.einsum("cxy,cn->nxy", pooled, head32, precision=HIGH)
    salt_exp = jnp.exp(capped(salt_raw))
    prob = salt_exp / jnp.sum(salt_exp, axis=0, keepdims=True)
    classes = jnp.arange(head.shape[1], dtype=jnp.int32)
    onehot = (labels[None] == classes[:, None, None]).astype(jnp.float32)
    dlog = (prob - onehot) * cap_slope(salt_raw) * scale
    dvec = jnp.einsum("cn,nxy->cxy", head32, dlog, precision=HIGH)
    attn = expo / total[:, None, :]
    along = jnp.einsum("cxy,cxzy->xzy", dvec, field32, precision=HIGH)
    inner = jnp.sum(dvec * pooled, axis=0)
    dscore = attn * (along - inner[:, None, :]) * cap_slope(raw)
    return (
        attn[None] * dvec[:, :, None, :]
        + dscore[None] * query.astype(jnp.float32)[:, None, None, None]
    )


def on_device(
    features,
    conv1_weight,
    conv2_weight,
    fault_head,
    horizon_head,
    salt_query,
    salt_head,
    fault_labels,
    horizon_labels,
    salt_labels,
):
    chans, inline_cells, depth_cells, cross_cells = features.shape
    tile_count = lax.axis_size(TILE)
    depth_total = depth_cells * tile_count
    scale = 1.0 / math.sqrt(inline_cells * lax.axis_size(INLINE) * depth_total * cross_cells)
    input_pad = pad_cross(padded_2(features, ((INLINE, 1), (TILE, 2)), D1), D1)
    first_pre = conv_local(
        input_pad[None], conv1_weight, D1, inline_cells, depth_cells, cross_cells
    )[0]
    first_out = (features.astype(jnp.float32) + jax.nn.silu(first_pre)).astype(jnp.bfloat16)
    hidden_pad = pad_cross(padded_2(first_out, ((INLINE, 1), (TILE, 2)), D2), D2)
    second_pre = conv_local(
        hidden_pad[None], conv2_weight, D2, inline_cells, depth_cells, cross_cells
    )[0]
    second_out = (first_out.astype(jnp.float32) + jax.nn.silu(second_pre)).astype(jnp.bfloat16)
    fault_cot = head_cotangent(second_out, fault_head, fault_labels, scale)
    horizon_cot = head_cotangent(second_out, horizon_head, horizon_labels, scale)
    columns = lax.all_to_all(second_out, TILE, split_axis=3, concat_axis=2, tiled=True)
    share = cross_cells // tile_count
    column_labels = lax.dynamic_slice_in_dim(salt_labels, lax.axis_index(TILE) * share, share, 1)
    raw, expo, num, total = trace_stats(columns, salt_query)
    column_cot = trace_backward(
        columns.astype(jnp.float32),
        raw,
        expo,
        num,
        total,
        salt_query,
        salt_head,
        column_labels,
        depth_total * scale,
    )
    salt_cot = lax.all_to_all(column_cot, TILE, split_axis=2, concat_axis=3, tiled=True)
    cot = jnp.stack([fault_cot, horizon_cot, salt_cot])
    second_delta = (cot * silu_slope(second_pre)[None]).astype(jnp.bfloat16)
    second_grad = weight_local(hidden_pad, second_delta, D2, inline_cells, depth_cells, cross_cells)
    delta_pad = pad_cross(padded_2(second_delta, ((INLINE, 2), (TILE, 3)), D2), D2)
    turned = conv2_weight[:, ::-1, :].transpose(2, 1, 0)
    first_cot = cot + conv_local(delta_pad, turned, D2, inline_cells, depth_cells, cross_cells)
    first_delta = (first_cot * silu_slope(first_pre)[None]).astype(jnp.bfloat16)
    first_grad = weight_local(input_pad, first_delta, D1, inline_cells, depth_cells, cross_cells)
    local_terms = (first_grad.reshape(3, -1), second_grad.reshape(3, -1))
    norm_count = 27 * chans * chans
    share_first, share_second = (
        lax.psum_scatter(local_terms[0], INLINE_TILE, scatter_dimension=1, tiled=True),
        lax.psum_scatter(local_terms[1], INLINE_TILE, scatter_dimension=1, tiled=True),
    )
    grads = jnp.stack([share_first, share_second])
    partial_gram = jnp.einsum("bti,bui->btu", grads, grads, precision=HIGH) / norm_count
    gram = by_axis(partial_gram, INLINE_TILE)
    return (grads, gram)


def solution(mesh):
    split = Mesh(
        mesh.devices.reshape(4, 2, 2, 4, 4), ("inline_0", "inline_1", "tile_0", "tile_1", "tile_2")
    )
    return jax.shard_map(
        on_device,
        mesh=split,
        in_specs=(
            P(None, INLINE, TILE, None),
            P(),
            P(),
            P(),
            P(),
            P(),
            P(),
            P(INLINE, TILE, None),
            P(INLINE, TILE, None),
            P(INLINE, None),
        ),
        out_specs=(P(None, None, INLINE_TILE), P()),
        check_vma=False,
    )
```

profile of v0, /device:TPU:1, one launch (start us, length us, event | category | flops | bytes accessed | tf_op | source)
XLA Modules:
  0.0 513.7 jit_solution(2545206493018555368)
XLA Ops:
  8.1 6.3 %collective-permute-start = (bf16[96,1,2,128]{3,0,2,1:T(8,128)(2,1)S(1)}, bf16[96,1,2,128]{3,0,2,1:T(8,128)(2,1)S(1)}, u32[]{:S(2)}, u32[]{:S(2)}) collective-permute-start(bf16[96,1,2,128]{3,0,2,1:T(8,128)(2,1)S(1)} %get-tuple-element.150), channel_id=1, source_target_pairs={{0,32},{32,64},{64,96},{96,128},{128,160},{160,192},{192,224},{1,3... | collective-permute-start | bytes 147464 | tf_op jit(solution)/shard_map/ppermute | solution.py:28
  14.4 1.9 collective-permute-start.1
  16.3 2.0 reverse_bitcast_fusion
  19.8 1.6 copy_bitcast_fusion
  21.4 3.1 collective-permute-start.2
  24.5 1.4 collective-permute-start.3
  26.6 3.4 collective-permute-done.3
  33.6 6.0 %collective-permute-start.4 = (bf16[96,2,2,128]{3,0,2,1:T(8,128)(2,1)S(1)}, bf16[96,2,2,128]{3,0,2,1:T(8,128)(2,1)S(1)}, u32[]{:S(2)}, u32[]{:S(2)}) collective-permute-start(bf16[96,2,2,128]{3,0,2,1:T(8,128)(2,1)S(1)} %get-tuple-element.153), channel_id=1, source_target_pairs={{0,32},{32,64},{64,96},{96,128},{128,160},{160,192},{192,224},{1,3... | collective-permute-start | bytes 294920 | tf_op jit(solution)/shard_map/ppermute | solution.py:28
  39.5 1.9 collective-permute-start.5
  41.9 4.4 collective-permute-done.5
  46.4 3.1 collective-permute-start.6
  49.6 1.3 collective-permute-start.7
  51.7 1.6 slice_bitcast_fusion.49
  53.3 4.0 collective-permute-done.7
  57.3 1.5 fusion.327
  59.5 1.1 convolution_bitcast_fusion.35
  60.6 1.1 convolution_bitcast_fusion.34
  61.7 1.1 convolution_bitcast_fusion.33
  62.9 1.1 convolution_bitcast_fusion.32
  64.0 1.1 convolution_bitcast_fusion.31
  65.1 1.1 convolution_bitcast_fusion.30
  66.2 1.1 convolution_bitcast_fusion.29
  67.3 1.1 convolution_bitcast_fusion.28
  68.5 1.1 convolution_bitcast_fusion.27
  70.6 14.2 %all-to-all-start = ((bf16[96,2,2,128]{0,2,1,3:T(2,128)(2,1)}), bf16[96,2,2,128]{0,2,1,3:T(2,128)(2,1)S(1)}, u32[]{:S(2)}, u32[]{:S(2)}) async-start(bf16[96,2,2,128]{0,2,1,3:T(2,128)(2,1)} %copy.191), calls=%async_computation | async-start | bytes 262144 | tf_op jit(solution)/shard_map/all_to_all | solution.py:170
  85.5 1.5 select_maximum_fusion.2
  88.4 3.8 all-to-all-done
  95.3 3.9 all-to-all-start.1
  99.6 1.5 slice_bitcast_fusion.26
  101.2 6.7 %all-to-all-done.1 = f32[96,2,64,4]{0,3,1,2:T(4,128)S(1)} async-done(((f32[96,2,64,4]{0,3,1,2:T(4,128)}), f32[96,2,64,4]{0,3,1,2:T(4,128)S(1)}, u32[]{:S(2)}, u32[]{:S(2)}) %all-to-all-start.1) | async-done | bytes 196640 | tf_op jit(solution)/shard_map/all_to_all | solution.py:185
  108.4 5.1 collective-permute-start.8
  113.5 1.9 collective-permute-start.9
  115.4 2.1 fusion.32
  117.5 1.1 fusion.31
  118.6 2.0 fusion.30
  120.6 2.0 fusion.29
  122.6 1.1 fusion.28
  124.5 1.1 fusion.27
  126.6 2.1 collective-permute-start.10
  128.8 1.3 collective-permute-start.11
  130.1 2.1 fusion.26
  132.2 2.0 fusion.25
  134.2 2.1 fusion.24
  136.3 6.7 %copy.221 = f32[3,96,27,96]{3,2,1,0:T(8,128)} copy(f32[3,96,27,96]{1,3,2,0:T(8,128)} %fusion.24) | data formatting | bytes 5971968 | tf_op jit(solution)/shard_map/concatenate | solution.py:101
  143.0 7.6 %reshape.155 = f32[3,248832]{1,0:T(4,128)} reshape(f32[3,96,27,96]{3,2,1,0:T(8,128)} %copy.221) | data formatting | bytes 5971968 | tf_op jit(solution)/shard_map/reshape | solution.py:194
  151.6 5.3 %select_maximum_fusion = bf16[3,96,6,6,132]{4,1,3,2,0:T(8,128)(2,1)S(1)} fusion(bf16[3,96,6,2,128]{4,1,3,2,0:T(8,128)(2,1)S(1)} %collective-permute-done.11, bf16[3,96,6,2,128]{4,1,3,2,0:T(8,128)(2,1)S(1)} %collective-permute-done.10, bf16[3,96,2,2,128]{4,1,3,2,0:T(8,128)(2,1)S(1)} %collective-permute-done.9, ...), kind=kLoop, calls=%fused_computation.6 | loop fusion | flops 24634368 | bytes 5391360 | tf_op jit(solution)/shard_map/concatenate | solution.py:30
  156.9 1.4 slice_bitcast_fusion.23
  163.1 1.1 fusion.41
  164.2 1.1 fusion.40
  165.3 1.1 fusion.39
  166.5 1.1 fusion.38
  167.6 1.1 fusion.37
  168.7 1.1 fusion.36
  169.8 1.1 fusion.35
  170.9 1.2 fusion.34
  172.1 1.1 fusion.33
  173.2 6.7 %copy.220 = f32[3,96,27,96]{3,2,1,0:T(8,128)} copy(f32[3,96,27,96]{1,3,2,0:T(8,128)} %fusion.33) | data formatting | bytes 5971968 | tf_op jit(solution)/shard_map/concatenate | solution.py:101
  179.9 7.6 %reshape.154 = f32[3,248832]{1,0:T(4,128)} reshape(f32[3,96,27,96]{3,2,1,0:T(8,128)} %copy.220) | data formatting | bytes 5971968 | tf_op jit(solution)/shard_map/reshape | solution.py:194
  187.5 283.1 %all-reduce.8.cloned.1.call-done = (f32[3,248832]{1,0:T(4,128)}, f32[3,248832]{1,0:T(4,128)}) async-done(((f32[3,248832]{1,0:T(4,128)}, f32[3,248832]{1,0:T(4,128)}), (f32[3,248832]{1,0:T(4,128)}, f32[3,248832]{1,0:T(4,128)})) %all-reduce.8.cloned.1.call-update) | async-done | bytes 5971984
  472.5 10.4 %psum.35 = f32[2,3,3]{2,1,0:T(4,128)S(1)} all-reduce(f32[2,3,3]{2,1,0:T(4,128)S(1)} %convolution_multiply_fusion.1), channel_id=1, replica_groups=mesh['inline_0'=4,'inline_1'=2,'tile_0'=2,'tile_1'=4,'tile_2'=4] {'inlin..., use_global_device_ids=true, to_apply=%region_7.8 | all-reduce | flops 18 | bytes 144 | tf_op jit(solution)/shard_map/psum | solution.py:35
  482.9 3.2 psum.36
  486.1 4.1 psum.37
  490.2 8.1 %psum.38 = f32[2,3,3]{2,1,0:T(4,128)S(1)} all-reduce(f32[2,3,3]{2,1,0:T(4,128)S(1)} %psum.37), channel_id=1, replica_groups=mesh['inline_0'=4,'inline_1'=2,'tile_0'=2,'tile_1'=4,'tile_2'=4] {'tile_1'}, use_global_device_ids=true, to_apply=%region_10.11 | all-reduce | flops 18 | bytes 144 | tf_op jit(solution)/shard_map/psum | solution.py:35
  498.3 7.3 %psum.39 = f32[2,3,3]{2,1,0:T(4,128)S(1)} all-reduce(f32[2,3,3]{2,1,0:T(4,128)S(1)} %psum.38), channel_id=1, replica_groups=mesh['inline_0'=4,'inline_1'=2,'tile_0'=2,'tile_1'=4,'tile_2'=4] {'tile_2'}, use_global_device_ids=true, to_apply=%region_11.12 | all-reduce | flops 18 | bytes 144 | tf_op jit(solution)/shard_map/psum | solution.py:35
  (183 shorter events, 25.9 us)
Async XLA Ops:
  7.2 77.7 %copy-start = (bf16[96,4]{0,1:T(4,128)(2,1)S(1)}, bf16[96,4]{0,1:T(4,128)(2,1)}, u32[]{:S(2)}) copy-start(bf16[96,4]{0,1:T(4,128)(2,1)} %param.14) | copy-start | bytes 2308
  8.1 11.6 %collective-permute-start = (bf16[96,1,2,128]{3,0,2,1:T(8,128)(2,1)S(1)}, bf16[96,1,2,128]{3,0,2,1:T(8,128)(2,1)S(1)}, u32[]{:S(2)}, u32[]{:S(2)}) collective-permute-start(bf16[96,1,2,128]{3,0,2,1:T(8,128)(2,1)S(1)} %get-tuple-element.150), channel_id=1, source_target_pairs={{0,32},{32,64},{64,96},{96,128},{128,160},{160,192},{192,224},{1,3... | collective-permute-start | bytes 147464 | tf_op jit(solution)/shard_map/ppermute | solution.py:28
  14.4 6.9 %collective-permute-start.1 = (bf16[96,1,2,128]{3,0,2,1:T(8,128)(2,1)S(1)}, bf16[96,1,2,128]{3,0,2,1:T(8,128)(2,1)S(1)}, u32[]{:S(2)}, u32[]{:S(2)}) collective-permute-start(bf16[96,1,2,128]{3,0,2,1:T(8,128)(2,1)S(1)} %get-tuple-element.149), channel_id=1, source_target_pairs={{32,0},{64,32},{96,64},{128,96},{160,128},{192,160},{224,192},{33,... | collective-permute-start | bytes 147464 | tf_op jit(solution)/shard_map/ppermute | solution.py:29
  21.4 5.3 %collective-permute-start.2 = (bf16[96,4,1,128]{3,0,2,1:T(8,128)(2,1)S(1)}, bf16[96,4,1,128]{3,0,2,1:T(8,128)(2,1)S(1)}, u32[]{:S(2)}, u32[]{:S(2)}) collective-permute-start(bf16[96,4,1,128]{3,0,2,1:T(8,128)(2,1)S(1)} %get-tuple-element.143), channel_id=1, source_target_pairs={{0,1},{1,2},{2,3},{3,4},{4,5},{5,6},{6,7},{7,8},{8,9},{9,10},{10,1... | collective-permute-start | bytes 294920 | tf_op jit(solution)/shard_map/ppermute | solution.py:28
  24.5 6.7 %copy-start.6 = (bf16[96,27,96]{2,0,1:T(8,128)(2,1)S(1)}, bf16[96,27,96]{2,0,1:T(8,128)(2,1)}, u32[]{:S(2)}) copy-start(bf16[96,27,96]{2,0,1:T(8,128)(2,1)} %param.11) | copy-start | bytes 1492996
  24.5 5.5 %collective-permute-start.3 = (bf16[96,4,1,128]{3,0,2,1:T(8,128)(2,1)S(1)}, bf16[96,4,1,128]{3,0,2,1:T(8,128)(2,1)S(1)}, u32[]{:S(2)}, u32[]{:S(2)}) collective-permute-start(bf16[96,4,1,128]{3,0,2,1:T(8,128)(2,1)S(1)} %get-tuple-element.144), channel_id=1, source_target_pairs={{1,0},{2,1},{3,2},{4,3},{5,4},{6,5},{7,6},{8,7},{9,8},{10,9},{11,1... | collective-permute-start | bytes 294920 | tf_op jit(solution)/shard_map/ppermute | solution.py:29
  31.2 2.1 copy-start.5
  33.6 8.4 %collective-permute-start.4 = (bf16[96,2,2,128]{3,0,2,1:T(8,128)(2,1)S(1)}, bf16[96,2,2,128]{3,0,2,1:T(8,128)(2,1)S(1)}, u32[]{:S(2)}, u32[]{:S(2)}) collective-permute-start(bf16[96,2,2,128]{3,0,2,1:T(8,128)(2,1)S(1)} %get-tuple-element.153), channel_id=1, source_target_pairs={{0,32},{32,64},{64,96},{96,128},{128,160},{160,192},{192,224},{1,3... | collective-permute-start | bytes 294920 | tf_op jit(solution)/shard_map/ppermute | solution.py:28
  39.5 6.8 %collective-permute-start.5 = (bf16[96,2,2,128]{3,0,2,1:T(8,128)(2,1)S(1)}, bf16[96,2,2,128]{3,0,2,1:T(8,128)(2,1)S(1)}, u32[]{:S(2)}, u32[]{:S(2)}) collective-permute-start(bf16[96,2,2,128]{3,0,2,1:T(8,128)(2,1)S(1)} %get-tuple-element.153), channel_id=1, source_target_pairs={{32,0},{64,32},{96,64},{128,96},{160,128},{192,160},{224,192},{33,... | collective-permute-start | bytes 294920 | tf_op jit(solution)/shard_map/ppermute | solution.py:29
  46.4 6.9 %collective-permute-start.6 = (bf16[96,6,2,128]{3,0,2,1:T(8,128)(2,1)S(1)}, bf16[96,6,2,128]{3,0,2,1:T(8,128)(2,1)S(1)}, u32[]{:S(2)}, u32[]{:S(2)}) collective-permute-start(bf16[96,6,2,128]{3,0,2,1:T(8,128)(2,1)S(1)} %pad_maximum_fusion.10), channel_id=1, source_target_pairs={{0,1},{1,2},{2,3},{3,4},{4,5},{5,6},{6,7},{7,8},{8,9},{9,10},{10,1... | collective-permute-start | bytes 884744 | tf_op jit(solution)/shard_map/ppermute | solution.py:28
  49.6 7.7 %collective-permute-start.7 = (bf16[96,6,2,128]{3,0,2,1:T(8,128)(2,1)S(1)}, bf16[96,6,2,128]{3,0,2,1:T(8,128)(2,1)S(1)}, u32[]{:S(2)}, u32[]{:S(2)}) collective-permute-start(bf16[96,6,2,128]{3,0,2,1:T(8,128)(2,1)S(1)} %pad_maximum_fusion.10), channel_id=1, source_target_pairs={{1,0},{2,1},{3,2},{4,3},{5,4},{6,5},{7,6},{8,7},{9,8},{10,9},{11,1... | collective-permute-start | bytes 884744 | tf_op jit(solution)/shard_map/ppermute | solution.py:29
  64.0 21.0 %copy-start.44 = (s32[2,2,128]{2,1,0:T(2,128)S(1)}, s32[2,2,128]{2,1,0:T(2,128)}, u32[]{:S(2)}) copy-start(s32[2,2,128]{2,1,0:T(2,128)} %param.18) | copy-start | bytes 6148
  64.0 21.3 %copy-start.42 = (bf16[96,2]{0,1:T(2,128)(2,1)S(1)}, bf16[96,2]{0,1:T(2,128)(2,1)}, u32[]{:S(2)}) copy-start(bf16[96,2]{0,1:T(2,128)(2,1)} %param.13) | copy-start | bytes 1156
  68.5 19.9 %copy-start.45 = (s32[2,2,128]{2,1,0:T(2,128)S(1)}, s32[2,2,128]{2,1,0:T(2,128)}, u32[]{:S(2)}) copy-start(s32[2,2,128]{2,1,0:T(2,128)} %param.17) | copy-start | bytes 6148
  69.6 22.8 %copy-start.43 = (bf16[96]{0:T(256)(128)(2,1)S(1)}, bf16[96]{0:T(256)(128)(2,1)}, u32[]{:S(2)}) copy-start(bf16[96]{0:T(256)(128)(2,1)} %param.15) | copy-start | bytes 580
  69.6 23.5 %copy-start.46 = (bf16[96,2]{0,1:T(2,128)(2,1)S(1)}, bf16[96,2]{0,1:T(2,128)(2,1)}, u32[]{:S(2)}) copy-start(bf16[96,2]{0,1:T(2,128)(2,1)} %param.16) | copy-start | bytes 1156
  70.6 21.6 %all-to-all-start = ((bf16[96,2,2,128]{0,2,1,3:T(2,128)(2,1)}), bf16[96,2,2,128]{0,2,1,3:T(2,128)(2,1)S(1)}, u32[]{:S(2)}, u32[]{:S(2)}) async-start(bf16[96,2,2,128]{0,2,1,3:T(2,128)(2,1)} %copy.191), calls=%async_computation | async-start | bytes 262144 | tf_op jit(solution)/shard_map/all_to_all | solution.py:170
  95.3 12.6 %all-to-all-start.1 = ((f32[96,2,64,4]{0,3,1,2:T(4,128)}), f32[96,2,64,4]{0,3,1,2:T(4,128)S(1)}, u32[]{:S(2)}, u32[]{:S(2)}) async-start(f32[96,2,64,4]{0,3,1,2:T(4,128)} %multiply_add_fusion), calls=%async_computation.1 | async-start | bytes 524288 | tf_op jit(solution)/shard_map/all_to_all | solution.py:185
  99.3 371.4 %all-reduce.8.cloned.1.call-start = ((), (), s32[]{:S(2)}) async-start(), calls=%async_computation.2 | async-start | bytes 15925248
  101.1 16.4 %copy-start.30 = (bf16[96,1,2,2,128]{4,0,3,2,1:T(8,128)(2,1)S(1)}, bf16[96,1,2,2,128]{4,0,3,2,1:T(8,128)(2,1)}, u32[]{:S(2)}) copy-start(bf16[96,1,2,2,128]{4,0,3,2,1:T(8,128)(2,1)} %get-tuple-element.45) | copy-start | bytes 294916
  101.1 16.4 %copy-start.31 = (bf16[96,1,2,2,128]{4,0,3,2,1:T(8,128)(2,1)S(1)}, bf16[96,1,2,2,128]{4,0,3,2,1:T(8,128)(2,1)}, u32[]{:S(2)}) copy-start(bf16[96,1,2,2,128]{4,0,3,2,1:T(8,128)(2,1)} %get-tuple-element.46) | copy-start | bytes 294916
  101.1 17.5 %copy-start.28 = (bf16[96,1,2,2,128]{4,0,3,2,1:T(8,128)(2,1)S(1)}, bf16[96,1,2,2,128]{4,0,3,2,1:T(8,128)(2,1)}, u32[]{:S(2)}) copy-start(bf16[96,1,2,2,128]{4,0,3,2,1:T(8,128)(2,1)} %get-tuple-element.43) | copy-start | bytes 294916
  101.2 17.5 %copy-start.29 = (bf16[96,1,2,2,128]{4,0,3,2,1:T(8,128)(2,1)S(1)}, bf16[96,1,2,2,128]{4,0,3,2,1:T(8,128)(2,1)}, u32[]{:S(2)}) copy-start(bf16[96,1,2,2,128]{4,0,3,2,1:T(8,128)(2,1)} %get-tuple-element.44) | copy-start | bytes 294916
  101.2 19.4 %copy-start.26 = (bf16[96,1,2,2,128]{4,0,3,2,1:T(8,128)(2,1)S(1)}, bf16[96,1,2,2,128]{4,0,3,2,1:T(8,128)(2,1)}, u32[]{:S(2)}) copy-start(bf16[96,1,2,2,128]{4,0,3,2,1:T(8,128)(2,1)} %get-tuple-element.41) | copy-start | bytes 294916
  101.2 19.4 %copy-start.27 = (bf16[96,1,2,2,128]{4,0,3,2,1:T(8,128)(2,1)S(1)}, bf16[96,1,2,2,128]{4,0,3,2,1:T(8,128)(2,1)}, u32[]{:S(2)}) copy-start(bf16[96,1,2,2,128]{4,0,3,2,1:T(8,128)(2,1)} %get-tuple-element.42) | copy-start | bytes 294916
  101.2 21.4 %copy-start.25 = (bf16[96,1,2,2,128]{4,0,3,2,1:T(8,128)(2,1)S(1)}, bf16[96,1,2,2,128]{4,0,3,2,1:T(8,128)(2,1)}, u32[]{:S(2)}) copy-start(bf16[96,1,2,2,128]{4,0,3,2,1:T(8,128)(2,1)} %get-tuple-element.40) | copy-start | bytes 294916
  108.3 16.2 %copy-start.32 = (bf16[96,1,2,2,128]{4,0,3,2,1:T(8,128)(2,1)S(1)}, bf16[96,1,2,2,128]{4,0,3,2,1:T(8,128)(2,1)}, u32[]{:S(2)}) copy-start(bf16[96,1,2,2,128]{4,0,3,2,1:T(8,128)(2,1)} %get-tuple-element.135) | copy-start | bytes 294916
  108.4 17.2 %collective-permute-start.8 = (bf16[3,96,2,2,128]{4,1,3,2,0:T(8,128)(2,1)S(1)}, bf16[3,96,2,2,128]{4,1,3,2,0:T(8,128)(2,1)S(1)}, u32[]{:S(2)}, u32[]{:S(2)}) collective-permute-start(bf16[3,96,2,2,128]{4,1,3,2,0:T(8,128)(2,1)S(1)} %multiply_convert_fusion), channel_id=1, source_target_pairs={{0,32},{32,64},{64,96},{96,128},{128,160},{160,192},{192,224},{1,3... | collective-permute-start | bytes 884744 | tf_op jit(solution)/shard_map/ppermute | solution.py:28
  113.5 12.2 %collective-permute-start.9 = (bf16[3,96,2,2,128]{4,1,3,2,0:T(8,128)(2,1)S(1)}, bf16[3,96,2,2,128]{4,1,3,2,0:T(8,128)(2,1)S(1)}, u32[]{:S(2)}, u32[]{:S(2)}) collective-permute-start(bf16[3,96,2,2,128]{4,1,3,2,0:T(8,128)(2,1)S(1)} %multiply_convert_fusion), channel_id=1, source_target_pairs={{32,0},{64,32},{96,64},{128,96},{160,128},{192,160},{224,192},{33,... | collective-permute-start | bytes 884744 | tf_op jit(solution)/shard_map/ppermute | solution.py:29
  125.6 1.0 copy-start.2
  126.6 24.9 %collective-permute-start.10 = (bf16[3,96,6,2,128]{4,1,3,2,0:T(8,128)(2,1)}, bf16[3,96,6,2,128]{4,1,3,2,0:T(8,128)(2,1)S(1)}, u32[]{:S(2)}, u32[]{:S(2)}) collective-permute-start(bf16[3,96,6,2,128]{4,1,3,2,0:T(8,128)(2,1)} %pad_maximum_fusion), channel_id=1, source_target_pairs={{0,1},{1,2},{2,3},{3,4},{4,5},{5,6},{6,7},{7,8},{8,9},{9,10},{10,1... | collective-permute-start | bytes 2654216 | tf_op jit(solution)/shard_map/ppermute | solution.py:28
  128.8 22.8 %collective-permute-start.11 = (bf16[3,96,6,2,128]{4,1,3,2,0:T(8,128)(2,1)}, bf16[3,96,6,2,128]{4,1,3,2,0:T(8,128)(2,1)S(1)}, u32[]{:S(2)}, u32[]{:S(2)}) collective-permute-start(bf16[3,96,6,2,128]{4,1,3,2,0:T(8,128)(2,1)} %pad_maximum_fusion), channel_id=1, source_target_pairs={{1,0},{2,1},{3,2},{4,3},{5,4},{6,5},{7,6},{8,7},{9,8},{10,9},{11,1... | collective-permute-start | bytes 2654216 | tf_op jit(solution)/shard_map/ppermute | solution.py:29
  156.9 1.5 copy-start.4
  158.3 1.0 copy-start.3
  162.1 0.9 copy-start.23
  162.1 0.9 copy-start.24
  162.1 1.0 copy-start.41
  162.1 2.1 copy-start.21
  162.1 2.1 copy-start.22
  162.1 2.1 copy-start.35
  162.1 3.2 copy-start.19
  162.1 3.2 copy-start.20
  162.1 3.2 copy-start.40
  162.2 4.3 copy-start.17
  162.2 4.3 copy-start.18
  162.2 4.3 copy-start.39
  162.8 4.7 copy-start.15
  162.8 4.7 copy-start.16
  162.9 4.7 copy-start.33
  162.9 5.8 %copy-start.13 = (bf16[96,1,2,2,128]{4,0,3,2,1:T(8,128)(2,1)S(1)}, bf16[96,1,2,2,128]{4,0,3,2,1:T(8,128)(2,1)}, u32[]{:S(2)}) copy-start(bf16[96,1,2,2,128]{4,0,3,2,1:T(8,128)(2,1)} %get-tuple-element.88) | copy-start | bytes 294916
  162.9 5.8 %copy-start.14 = (bf16[96,1,2,2,128]{4,0,3,2,1:T(8,128)(2,1)S(1)}, bf16[96,1,2,2,128]{4,0,3,2,1:T(8,128)(2,1)}, u32[]{:S(2)}) copy-start(bf16[96,1,2,2,128]{4,0,3,2,1:T(8,128)(2,1)} %get-tuple-element.89) | copy-start | bytes 294916
  162.9 5.8 %copy-start.38 = (bf16[96,1,2,2,128]{4,0,3,2,1:T(8,128)(2,1)S(1)}, bf16[96,1,2,2,128]{4,0,3,2,1:T(8,128)(2,1)}, u32[]{:S(2)}) copy-start(bf16[96,1,2,2,128]{4,0,3,2,1:T(8,128)(2,1)} %get-tuple-element.130) | copy-start | bytes 294916
  163.1 6.7 %copy-start.11 = (bf16[96,1,2,2,128]{4,0,3,2,1:T(8,128)(2,1)S(1)}, bf16[96,1,2,2,128]{4,0,3,2,1:T(8,128)(2,1)}, u32[]{:S(2)}) copy-start(bf16[96,1,2,2,128]{4,0,3,2,1:T(8,128)(2,1)} %get-tuple-element.86) | copy-start | bytes 294916
  163.1 6.8 %copy-start.12 = (bf16[96,1,2,2,128]{4,0,3,2,1:T(8,128)(2,1)S(1)}, bf16[96,1,2,2,128]{4,0,3,2,1:T(8,128)(2,1)}, u32[]{:S(2)}) copy-start(bf16[96,1,2,2,128]{4,0,3,2,1:T(8,128)(2,1)} %get-tuple-element.87) | copy-start | bytes 294916
  163.1 6.8 %copy-start.37 = (bf16[96,1,2,2,128]{4,0,3,2,1:T(8,128)(2,1)S(1)}, bf16[96,1,2,2,128]{4,0,3,2,1:T(8,128)(2,1)}, u32[]{:S(2)}) copy-start(bf16[96,1,2,2,128]{4,0,3,2,1:T(8,128)(2,1)} %get-tuple-element.142) | copy-start | bytes 294916
  164.2 6.8 %copy-start.9 = (bf16[96,1,2,2,128]{4,0,3,2,1:T(8,128)(2,1)S(1)}, bf16[96,1,2,2,128]{4,0,3,2,1:T(8,128)(2,1)}, u32[]{:S(2)}) copy-start(bf16[96,1,2,2,128]{4,0,3,2,1:T(8,128)(2,1)} %get-tuple-element.84) | copy-start | bytes 294916
  164.2 6.8 %copy-start.10 = (bf16[96,1,2,2,128]{4,0,3,2,1:T(8,128)(2,1)S(1)}, bf16[96,1,2,2,128]{4,0,3,2,1:T(8,128)(2,1)}, u32[]{:S(2)}) copy-start(bf16[96,1,2,2,128]{4,0,3,2,1:T(8,128)(2,1)} %get-tuple-element.85) | copy-start | bytes 294916
  164.2 6.8 %copy-start.34 = (bf16[96,1,2,2,128]{4,0,3,2,1:T(8,128)(2,1)S(1)}, bf16[96,1,2,2,128]{4,0,3,2,1:T(8,128)(2,1)}, u32[]{:S(2)}) copy-start(bf16[96,1,2,2,128]{4,0,3,2,1:T(8,128)(2,1)} %get-tuple-element.145) | copy-start | bytes 294916
  165.3 6.8 %copy-start.7 = (bf16[96,1,2,2,128]{4,0,3,2,1:T(8,128)(2,1)S(1)}, bf16[96,1,2,2,128]{4,0,3,2,1:T(8,128)(2,1)}, u32[]{:S(2)}) copy-start(bf16[96,1,2,2,128]{4,0,3,2,1:T(8,128)(2,1)} %get-tuple-element.83) | copy-start | bytes 294916
  165.3 6.8 %copy-start.8 = (bf16[96,1,2,2,128]{4,0,3,2,1:T(8,128)(2,1)S(1)}, bf16[96,1,2,2,128]{4,0,3,2,1:T(8,128)(2,1)}, u32[]{:S(2)}) copy-start(bf16[96,1,2,2,128]{4,0,3,2,1:T(8,128)(2,1)} %get-tuple-element.100) | copy-start | bytes 294916
  165.3 6.8 %copy-start.36 = (bf16[96,1,2,2,128]{4,0,3,2,1:T(8,128)(2,1)S(1)}, bf16[96,1,2,2,128]{4,0,3,2,1:T(8,128)(2,1)}, u32[]{:S(2)}) copy-start(bf16[96,1,2,2,128]{4,0,3,2,1:T(8,128)(2,1)} %get-tuple-element.128) | copy-start | bytes 294916
  187.5 319.3 %copy-start.1 = (bf16[96,4]{0,1:T(4,128)(2,1)S(1)}, bf16[96,4]{0,1:T(4,128)(2,1)}, u32[]{:S(2)}) copy-start(bf16[96,4]{0,1:T(4,128)(2,1)} %param.14) | copy-start | bytes 2308
Sparse Core Ops, SparseCore 0:
  187.6 282.9 all-reduce.7
where the time goes:
time: 519 us; the launch traced here: 514 us
  waiting for transfers between devices  306 us (59%)
  starting transfers between devices  53.7 us (10%)
  local copies, waits for them, and re-layouts  47.4 us (9%)
  matrix products  43.8 us (8%)
  blocking collectives  33.1 us (6%)
  other arithmetic  15.1 us (3%)
  between operations  15 us (3%)
    unnamed x2, waiting for transfers between devices  283 us
    psum x5, blocking collectives, by_axis(): return functools.reduce(lax.psum, axes, x)  33.1 us
    ppermute x6, starting transfers between devices, padded_2(): before = lax.ppermute(last, axis, up)  25.7 us
    dot_general x18, matrix products, weight_local(): jnp.einsum('ikxzy,toxzy->tiko', taps, deltas, preferred_element_type=jnp....  25.7 us
    dot_general x27, matrix products, conv_local(): jnp.einsum('ikd,bikxzy->bdxzy', kernel, taps, preferred_element_type=jnp....  15.9 us
    reshape x2, local copies, waits for them, and re-layouts, on_device(): local_terms = (first_grad.reshape(3, -1), second_grad.reshape(3, -1))  15.2 us
    all_to_all x1, starting transfers between devices, on_device(): lax.all_to_all(second_out, TILE, split_axis=3, concat_axis=2, tiled=True)  14.2 us
    concatenate x2, local copies, waits for them, and re-layouts, weight_local(): return jnp.concatenate(pieces, axis=2)  13.3 us
  transfers between devices with their start and end apart: 15, of which 6 were waited for; matrix products, arithmetic and copies ran while one was open for 9% of the time, Pallas kernels for 0%

commit v1 on v0

v1 whole, which is shorter than its diff:
```python
import functools
import math

import jax
import jax.numpy as jnp
import numpy as np
from jax import lax
from jax.experimental import pallas as pl
from jax.experimental.pallas import tpu as pltpu
from jax.sharding import Mesh
from jax.sharding import PartitionSpec as P

MESH = pl.DeviceIdType.MESH
TILE = ("tile_0", "tile_1", "tile_2")
INLINE = ("inline_0", "inline_1")
INLINE_TILE = INLINE + TILE
D1 = 1
D2 = 2
C = 96
V = 512
CAPPING = 8.0
F32 = jnp.float32
BF16 = jnp.bfloat16
LANES = 896
HALF = 512
NORM = 27 * C * C


def row_order():
    out = np.zeros((2, HALF, 9 * C), np.float32)
    for core in range(2):
        for half in range(2):
            for first in range(4):
                for second in range(4):
                    x, y = (first, second) if half == 0 else (second, first)
                    for z in range(8):
                        for r in range(2):
                            rho = (((y % 2) * 4 + x) * 2 + half) * 2 + r
                            if rho >= 27:
                                continue
                            s, ab = divmod(rho, 9)
                            i = 12 * ((z // 2) * 2 + core) + 3 * ((z % 2) * 2 + y // 2) + s
                            row = (((half * 4 + first) * 4 + second) * 8 + z) * 2 + r
                            out[core, row, ab * C + i] = 1.0
    return out


def shifted(x, k):
    lane = lax.broadcasted_iota(jnp.int32, (x.shape[0], 128), 1) + k
    keep = (lane >= 0) & (lane < 128)
    parts = []
    for j in range(x.shape[1] // 128):
        part = pltpu.roll(x[:, j * 128 : (j + 1) * 128], (-k) % 128, 1)
        parts.append(jnp.where(keep, part, 0.0))
    return jnp.concatenate(parts, axis=1)


def dot(a, b):
    return lax.dot_general(a, b, (((1,), (0,)), ((), ())), preferred_element_type=F32)


def dot_t(a, b):
    return lax.dot_general(a, b, (((1,), (1,)), ((), ())), preferred_element_type=F32)


def capped(value):
    return CAPPING * jnp.tanh(value / CAPPING)


def cap_slope(value):
    squash = jnp.tanh(value / CAPPING)
    return 1.0 - squash * squash


def head_logits(raw, labels, scale):
    expo = [jnp.exp(capped(r)) for r in raw]
    total = functools.reduce(lambda a, b: a + b, expo)
    return [
        (e / total - (labels == n).astype(F32)) * cap_slope(r) * scale
        for n, (e, r) in enumerate(zip(expo, raw))
    ]


def three_parts(g):
    hi = g.astype(BF16)
    rest = g - hi.astype(F32)
    mid = rest.astype(BF16)
    low = (rest - mid.astype(F32)).astype(BF16)
    return jnp.concatenate([hi, mid, low], axis=0)


def kernel(
    scale,
    depth_scale,
    feat_ref,
    w1_ref,
    w2_ref,
    w2t_ref,
    heads_ref,
    spread_ref,
    order_ref,
    fault_ref,
    horizon_ref,
    salt_ref,
    out_ref,
    gram_ref,
    fpad,
    f91,
    f92,
    slope9,
    g9,
    d9,
    slope1,
    cotc,
    amat,
    fsend,
    draw,
    dpart,
    dsh,
    pbuf,
    o32,
    s1src,
    s1recv,
    s2src,
    s2recv,
    r16,
    s3src,
    s3recv,
    tbuf,
    pool_x,
    pool_mine,
    pool_z,
    gram_x,
    gram_z,
    ssem,
    rsem,
):
    zh, core, zl, y, x = [lax.axis_index(a) for a in INLINE_TILE]
    inline = zh * 2 + core
    tile = zl * 16 + y * 4 + x
    z = zh * 2 + zl
    xy = y * 4 + x
    zc = z * 2 + core
    yhi, ylo = y // 2, y % 2
    p = ylo * 4 + x

    sem_count = [0]
    sent = []

    def send(src, dst, device):
        n = sem_count[0]
        sem_count[0] += 1
        copy = pltpu.make_async_remote_copy(
            src_ref=src,
            dst_ref=dst,
            send_sem=ssem.at[n],
            recv_sem=rsem.at[n],
            device_id=device,
            device_id_type=MESH,
        )
        copy.start()
        sent.append(copy)
        return copy

    def at_grid(dx, dz):
        i = (inline + dx + 8) % 8
        t = (tile + dz + 32) % 32
        return (i // 2, i % 2, t // 16, (t // 4) % 4, t % 4)

    around = [(dx, dz) for dx in (-1, 0, 1) for dz in (-1, 0, 1) if (dx, dz) != (0, 0)]
    halo_to = {d: at_grid(*d) for d in around}

    def plane(k):
        q = (xy + k) % 16
        return (zh, core, zl, q // 4, q % 4)

    def column(k):
        q = (zc + k) % 16
        return (q // 4, q % 2, (q // 2) % 2, y, x)

    partner = (zh, 1 - core, zl, y, x)

    for li in range(2):
        s3src[li] = jnp.zeros(s3src.shape[1:], F32)
    dsh[864:896, :] = jnp.zeros((32, 1024), BF16)

    for cell in range(4):
        fpad[(cell // 2 + 1) * 4 + cell % 2 + 1] = feat_ref[cell]

    barrier = pltpu.get_barrier_semaphore()
    greeted = [halo_to[d] for d in around] + [plane(k) for k in range(1, 16)]
    greeted += [column(k) for k in range(1, 16)]
    for device in greeted:
        pl.semaphore_signal(barrier, inc=1, device_id=device, device_id_type=MESH)
    pl.semaphore_wait(barrier, len(greeted))

    copies = []
    for dx, dz in around:
        for cx in (0, 1) if dx == 0 else ((1,) if dx == 1 else (0,)):
            for cz in (0, 1) if dz == 0 else ((1,) if dz == 1 else (0,)):
                src = (cx + 1) * 4 + cz + 1
                dst = (cx - 2 * dx + 1) * 4 + (cz - 2 * dz + 1)
                copies.append(send(fpad.at[src], fpad.at[dst], halo_to[dx, dz]))
    for copy in copies:
        copy.wait_recv()

    low_x, high_x = inline == 0, inline == 7
    low_z, high_z = tile == 0, tile == 31
    none = jnp.zeros((C, 128), BF16)

    @pl.when(low_x)
    def _():
        for j in range(4):
            fpad[j] = none

    @pl.when(high_x)
    def _():
        for j in range(4):
            fpad[12 + j] = none

    @pl.when(low_z)
    def _():
        for j in range(4):
            fpad[4 * j] = none

    @pl.when(high_z)
    def _():
        for j in range(4):
            fpad[4 * j + 3] = none

    for a in range(3):
        for b in range(3):
            for cell in range(4):
                row = (a * 3 + b) * C
                f91[row : row + C, cell * 128 : (cell + 1) * 128] = fpad[
                    (cell // 2 + a) * 4 + cell % 2 + b
                ]

    def taps_added(pbuf, d):
        return pbuf[C : 2 * C, :] + shifted(pbuf[0:C, :], -d) + shifted(pbuf[2 * C :, :], d)

    pbuf[...] = dot(w1_ref[...], f91[...])
    pre = taps_added(pbuf, D1)
    sig = jax.nn.sigmoid(pre)
    own = jnp.concatenate([feat_ref[cell] for cell in range(4)], axis=1).astype(F32)
    f92[4] = (own + pre * sig).astype(BF16)
    slope1[...] = sig * (1.0 + pre * (1.0 - sig))

    def blocks_around(buffer):
        made = []
        for dx, dz in around:
            slot = (1 - dx) * 3 + (1 - dz)
            made.append(send(buffer.at[4], buffer.at[slot], halo_to[dx, dz]))
        return made

    def clear_outside(buffer):
        zeros = jnp.zeros(buffer.shape[1:], buffer.dtype)

        @pl.when(low_x)
        def _():
            for j in range(3):
                buffer[j] = zeros

        @pl.when(high_x)
        def _():
            for j in range(3):
                buffer[6 + j] = zeros

        @pl.when(low_z)
        def _():
            for j in range(3):
                buffer[3 * j] = zeros

        @pl.when(high_z)
        def _():
            for j in range(3):
                buffer[3 * j + 2] = zeros

    def rows_exchanged(li, field):
        amat[li, :, 0:V] = dot(order_ref[core], field).astype(BF16)
        fsend[li] = dot(order_ref[1 - core], field).astype(BF16)
        return send(fsend.at[li], amat.at[li, :, V : 2 * V], partner)

    copies = blocks_around(f92)
    row_copy = [rows_exchanged(0, f91[...])]
    for copy in copies:
        copy.wait_recv()
    clear_outside(f92)

    field9 = f92[...].reshape(9 * C, V)
    pbuf[...] = dot(w2_ref[...], field9)
    pre = taps_added(pbuf, D2)
    sig = jax.nn.sigmoid(pre)
    second = (f92[4].astype(F32) + pre * sig).astype(BF16)
    slope2 = sig * (1.0 + pre * (1.0 - sig))
    slope9[4] = slope2.astype(BF16)
    slope_copies = blocks_around(slope9)

    raw = dot(heads_ref[...], second)
    rows = [raw[n : n + 1, :] for n in range(9)]
    expo = jnp.exp(capped(rows[6]))

    def depth_sum(r):
        return jnp.concatenate(
            [r[:, 0:128] + r[:, 128:256], r[:, 256:384] + r[:, 384:512]], axis=1
        )

    zero_row = jnp.zeros((1, 256), F32)
    partial = [depth_sum(expo), depth_sum(expo * rows[7]), depth_sum(expo * rows[8])]
    pool_x[xy] = jnp.concatenate(partial + [zero_row] * 5, axis=0)
    copies = [send(pool_x.at[xy], pool_x.at[xy], plane(k)) for k in range(1, 16)]
    logits = head_logits(rows[0:2], fault_ref[...], scale)
    logits += head_logits(rows[2:6], horizon_ref[...], scale)
    row_copy.append(rows_exchanged(1, field9))
    for copy in copies:
        copy.wait_recv()
    pooled = pool_x[0]
    for j in range(1, 16):
        pooled = pooled + pool_x[j]
    pool_mine[...] = pooled
    copy = send(pool_mine, pool_z, (zh, core, 1 - zl, y, x))
    copy.wait_recv()
    pooled = pool_mine[...] + pool_z[...]
    total = pooled[0:1, :]
    salt_raw = [pooled[1:2, :] / total, pooled[2:3, :] / total]
    salt_log = head_logits(salt_raw, salt_ref[...], depth_scale)
    inner = salt_log[0] * salt_raw[0] + salt_log[1] * salt_raw[1]

    def per_cell(r):
        return jnp.concatenate([r[:, 0:128], r[:, 0:128], r[:, 128:256], r[:, 128:256]], axis=1)

    attn = expo / per_cell(total)
    wide = [per_cell(r) for r in salt_log]
    along = wide[0] * rows[7] + wide[1] * rows[8]
    dscore = attn * (along - per_cell(inner)) * cap_slope(rows[6])
    voxel = logits + [dscore, attn * wide[0], attn * wide[1]]
    g = jnp.concatenate(voxel + [jnp.zeros((7, V), F32)], axis=0)
    g9[4] = g
    g_copies = blocks_around(g9)

    cot = dot(spread_ref[...], three_parts(g))
    cotc[...] = cot
    for t in range(3):
        delta = (cot[t * C : (t + 1) * C, :] * slope2).astype(BF16)
        d9[t, 4 * C : 5 * C, :] = delta
        draw[1, t * C : (t + 1) * C, :] = delta

    def shifted_deltas(ref, at, d):
        for t in range(3):
            mid = ref[t * C : (t + 1) * C, :]
            wide = mid.astype(F32)
            low = shifted(wide, d).astype(BF16)
            high = shifted(wide, -d).astype(BF16)
            cols = slice(at, at + V)
            dsh[t * 256 : t * 256 + 96, cols] = low
            dsh[t * 256 + 96 : t * 256 + 192, cols] = mid
            dsh[t * 256 + 192 : t * 256 + 256, cols] = high[0:64, :]
            dsh[768 + 32 * t : 800 + 32 * t, cols] = high[64:96, :]

    def at_x(k):
        return (zh, core, zl, y, (x + k) % 4)

    def at_y(k):
        return (zh, core, zl, (y + k) % 4, x)

    first_at, first_of = (at_x, at_y), (x, y)
    second_at, second_of = (at_y, at_x), (y, x)

    def stage1(li, d, delta_copy):
        shifted_deltas(draw.at[li], 0, d)
        delta_copy.wait_recv()
        shifted_deltas(dpart.at[li], V, d)
        row_copy[li].wait_recv()
        made = []
        for h in range(2):
            part = slice(h * 256, (h + 1) * 256)
            prod = dot_t(amat[li, part, :], dsh[...])
            o32[li, part, :] = prod
            s1src[li, part, :] = prod.astype(BF16)
            for k in range(1, 4):
                to = h * 256 + ((first_of[h] + k) % 4) * 64
                src = s1src.at[li, pl.ds(pl.multiple_of(to, 64), 64), :]
                made.append(send(src, s1recv.at[li, h, k - 1], first_at[h](k)))
        return made

    def stage2(li, copies):
        for copy in copies:
            copy.wait_recv()
        made = []
        for h in range(2):
            mine = pl.multiple_of(h * 256 + first_of[h] * 64, 64)
            part = o32[li, pl.ds(mine, 64), :]
            for k in range(3):
                part = part + s1recv[li, h, k].astype(F32)
            s2src[li, h] = part
            for k in range(1, 4):
                to = pl.multiple_of(((second_of[h] + k) % 4) * 16, 16)
                src = s2src.at[li, h, pl.ds(to, 16), :]
                made.append(send(src, s2recv.at[li, h, k - 1], second_at[h](k)))
        return made

    def stage3(li, copies):
        for copy in copies:
            copy.wait_recv()
        for h in range(2):
            mine = pl.multiple_of(second_of[h] * 16, 16)
            part = s2src[li, h, pl.ds(mine, 16), :]
            for k in range(3):
                part = part + s2recv[li, h, k]
            r16[...] = part
            for zz in range(8):
                for r in range(2):
                    row = zz * 2 + r
                    for lane in range(7):
                        s3src[li, zz, h * 2 + r, lane : lane + 1, :] = r16[
                            row : row + 1, lane * 128 : (lane + 1) * 128
                        ]
        made = []
        for k in range(1, 8):
            q = (z + k) % 8
            made.append(send(s3src.at[li, q], s3recv.at[li, k - 1], (q // 2, core, q % 2, y, x)))
        return made

    def stage4(li, copies):
        for copy in copies:
            copy.wait_recv()
        part = s3src[li, z]
        for k in range(7):
            part = part + s3recv[li, k]
        tbuf[li, p] = part
        made = []
        for k in range(1, 8):
            q = (p + k) % 8
            device = (zh, core, zl, yhi * 2 + q // 4, q % 4)
            made.append(send(tbuf.at[li, p], tbuf.at[li, p], device))
        return part, made

    def gram_rows(part):
        lane = lax.broadcasted_iota(jnp.int32, (4, 128), 1)
        tail = part[:, 6, :]
        values = []
        for t in range(3):
            rest = tail if t == 0 else pltpu.roll(tail, 128 - 32 * t, 1)
            rest = jnp.where(lane < 32, rest, 0.0)
            values.append((part[:, 2 * t, :], part[:, 2 * t + 1, :], rest))
        found = []
        for t in range(3):
            for u in range(t, 3):
                prod = sum(a * b for a, b in zip(values[t], values[u]))
                found.append(jnp.sum(prod, axis=0, keepdims=True))
        return found

    copy = send(draw.at[1], dpart.at[1], partner)
    reduce2 = stage1(1, D2, copy)

    for copy in slope_copies:
        copy.wait_recv()
    clear_outside(slope9)
    for copy in g_copies:
        copy.wait_recv()
    for s in range(9):
        if s == 4:
            continue
        cot = dot(spread_ref[...], three_parts(g9[s]))
        slope = slope9[s].astype(F32)
        for t in range(3):
            d9[t, (8 - s) * C : (9 - s) * C, :] = (cot[t * C : (t + 1) * C, :] * slope).astype(
                BF16
            )
    for t in range(3):
        pbuf[...] = dot(w2t_ref[...], d9[t])
        cot = cotc[t * C : (t + 1) * C, :] + taps_added(pbuf, -D2)
        draw[0, t * C : (t + 1) * C, :] = (cot * slope1[...]).astype(BF16)
    copy = send(draw.at[0], dpart.at[0], partner)
    reduce2 = stage2(1, reduce2)
    reduce1 = stage1(0, D1, copy)
    reduce2 = stage3(1, reduce2)
    reduce1 = stage2(0, reduce1)
    part2, spread2 = stage4(1, reduce2)
    found2 = gram_rows(part2)
    reduce1 = stage3(0, reduce1)
    part1, spread1 = stage4(0, reduce1)
    found = gram_rows(part1) + found2 + [jnp.zeros((4, 128), F32)]
    gram_x[xy] = jnp.concatenate(found, axis=0)
    copies = [send(gram_x.at[xy], gram_x.at[xy], plane(k)) for k in range(1, 16)]
    for copy in copies:
        copy.wait_recv()
    part = gram_x[0]
    for j in range(1, 16):
        part = part + gram_x[j]
    gram_z[zc] = part
    copies = [send(gram_z.at[zc], gram_z.at[zc], column(k)) for k in range(1, 16)]
    for copy in spread2 + spread1:
        copy.wait_recv()
    out_ref[...] = tbuf[...]
    for copy in copies:
        copy.wait_recv()
    part = gram_z[0]
    for j in range(1, 16):
        part = part + gram_z[j]
    gram_ref[...] = part
    for copy in sent:
        copy.wait_send()


def on_device(
    features,
    conv1_weight,
    conv2_weight,
    fault_head,
    horizon_head,
    salt_query,
    salt_head,
    fault_labels,
    horizon_labels,
    salt_labels,
):
    chans, inline_cells, depth_cells, cross_cells = features.shape
    depth_total = depth_cells * lax.axis_size(TILE)
    scale = 1.0 / math.sqrt(inline_cells * lax.axis_size(INLINE) * depth_total * cross_cells)
    cells = features.transpose(1, 2, 0, 3).reshape(4, C, 128)
    w1 = conv1_weight.reshape(C, 9, 3, C).transpose(2, 3, 1, 0).reshape(3 * C, 9 * C)
    w2 = conv2_weight.reshape(C, 9, 3, C).transpose(2, 3, 1, 0).reshape(3 * C, 9 * C)
    w2t = conv2_weight.reshape(C, 9, 3, C).transpose(2, 0, 1, 3).reshape(3 * C, 9 * C)
    heads = jnp.concatenate(
        [fault_head, horizon_head, salt_query[:, None], salt_head, jnp.zeros((C, 7), BF16)], axis=1
    )
    task = np.zeros((3, 16), np.float32)
    task[0, 0:2] = 1.0
    task[1, 2:6] = 1.0
    task[2, 6:9] = 1.0
    spread = (heads[None] * jnp.asarray(task, BF16)[:, None, :]).reshape(3 * C, 16)
    spread = jnp.concatenate([spread] * 3, axis=1)
    order = jnp.asarray(row_order(), BF16)

    scratch = [
        pltpu.VMEM((16, C, 128), BF16),
        pltpu.VMEM((9 * C, V), BF16),
        pltpu.VMEM((9, C, V), BF16),
        pltpu.VMEM((9, C, V), BF16),
        pltpu.VMEM((9, 16, V), F32),
        pltpu.VMEM((3, 9 * C, V), BF16),
        pltpu.VMEM((C, V), F32),
        pltpu.VMEM((3 * C, V), F32),
        pltpu.VMEM((2, HALF, 2 * V), BF16),
        pltpu.VMEM((2, HALF, V), BF16),
        pltpu.VMEM((2, 3 * C, V), BF16),
        pltpu.VMEM((2, 3 * C, V), BF16),
        pltpu.VMEM((LANES, 2 * V), BF16),
        pltpu.VMEM((3 * C, V), F32),
        pltpu.VMEM((2, HALF, LANES), F32),
        pltpu.VMEM((2, HALF, LANES), BF16),
        pltpu.VMEM((2, 2, 3, 64, LANES), BF16),
        pltpu.VMEM((2, 2, 64, LANES), F32),
        pltpu.VMEM((2, 2, 3, 16, LANES), F32),
        pltpu.VMEM((16, LANES), F32),
        pltpu.VMEM((2, 8, 4, 8, 128), F32),
        pltpu.VMEM((2, 7, 4, 8, 128), F32),
        pltpu.VMEM((2, 8, 4, 8, 128), F32),
        pltpu.VMEM((16, 8, 256), F32),
        pltpu.VMEM((8, 256), F32),
        pltpu.VMEM((8, 256), F32),
        pltpu.VMEM((16, 16, 128), F32),
        pltpu.VMEM((16, 16, 128), F32),
        pltpu.SemaphoreType.DMA((160,)),
        pltpu.SemaphoreType.DMA((160,)),
    ]
    whole = pl.BlockSpec(memory_space=pltpu.VMEM)
    units, gram_rows = pl.pallas_call(
        functools.partial(kernel, scale, depth_total * scale),
        out_shape=(
            jax.ShapeDtypeStruct((2, 8, 4, 8, 128), F32),
            jax.ShapeDtypeStruct((16, 128), F32),
        ),
        in_specs=[whole] * 10,
        out_specs=(whole, whole),
        scratch_shapes=scratch,
        compiler_params=pltpu.CompilerParams(
            collective_id=0, has_side_effects=True, vmem_limit_bytes=48 * 1024 * 1024
        ),
    )(
        cells,
        w1,
        w2,
        w2t,
        heads.T,
        spread,
        order,
        fault_labels.reshape(1, V),
        horizon_labels.reshape(1, V),
        salt_labels.reshape(1, 256),
    )
    p = (lax.axis_index("tile_1") % 2) * 4 + lax.axis_index("tile_2")
    start = (27 * p) // 8
    mine = lax.dynamic_slice_in_dim(units.reshape(2, 32, 1024), start, 5, 1)
    main = mine[:, :, 0:768].reshape(2, 5, 3, 256)
    tail = mine[:, :, 768:864].reshape(2, 5, 3, 32)
    entries = jnp.concatenate([main, tail], axis=3).transpose(0, 2, 1, 3).reshape(2, 3, 5 * 288)
    grads = lax.dynamic_slice_in_dim(entries, 36 * ((27 * p) % 8), NORM // 256, 2)
    sums = jnp.sum(gram_rows[0:12, :], axis=1).reshape(2, 6) / NORM
    gram = sums[:, np.array([0, 1, 2, 1, 3, 4, 2, 4, 5])].reshape(2, 3, 3)
    return (grads, gram)


def solution(mesh):
    split = Mesh(
        mesh.devices.reshape(4, 2, 2, 4, 4), ("inline_0", "inline_1", "tile_0", "tile_1", "tile_2")
    )
    return jax.shard_map(
        on_device,
        mesh=split,
        in_specs=(
            P(None, INLINE, TILE, None),
            P(),
            P(),
            P(),
            P(),
            P(),
            P(),
            P(INLINE, TILE, None),
            P(INLINE, TILE, None),
            P(INLINE, None),
        ),
        out_specs=(P(None, None, INLINE_TILE), P()),
        check_vma=False,
    )
```

time: 519 us -> 110 us (0.21); the launches traced: 514 us -> 110 us
  waiting for transfers between devices: 306 us -> 0 us
  Pallas kernels: 0 us -> 92.5 us
  starting transfers between devices: 53.7 us -> 0 us
  matrix products: 43.8 us -> 0 us
  blocking collectives: 33.1 us -> 0 us
  local copies, waits for them, and re-layouts: 47.4 us -> 16.5 us
  other arithmetic: 15.1 us -> 0.26 us
  between operations: 15 us -> 0.96 us
    unnamed x2 -> x0, waiting for transfers between devices: 283 us -> none
    pallas_call x0 -> x1, Pallas kernels: none -> 92.5 us  [on_device(): pl.pallas_call(functools.partial(kernel, scale, depth_total * scale), out...]
    dot_general x55 -> x0, matrix products: 43.8 us -> none  [the longest x18 25.7 us: weight_local(): jnp.einsum('ikxzy,toxzy->tiko', taps, deltas, preferred_element_type=jnp....]
    ppermute x12 -> x0, starting transfers between devices: 35.5 us -> none  [the longest x6 25.7 us: padded_2(): before = lax.ppermute(last, axis, up)]
    psum x5 -> x0, blocking collectives: 33.1 us -> none  [by_axis(): return functools.reduce(lax.psum, axes, x)]
    all_to_all x2 -> x0, starting transfers between devices: 18.2 us -> none  [the longest x1 14.2 us: on_device(): lax.all_to_all(second_out, TILE, split_axis=3, concat_axis=2, tiled=True)]
    concatenate x3 -> x2, local copies, waits for them, and re-layouts: 13.3 us -> 0.25 us  [on_device(): jnp.concatenate([fault_head, horizon_head, salt_query[:, None], salt_head...]
    ppermute x12 -> x0, waiting for transfers between devices: 11.8 us -> none  [the longest x6 11.8 us: padded_2(): after = lax.ppermute(initial, axis, down)]
  transfers between devices with their start and end apart: 15 -> 0, of which waited for: 6 -> 0; matrix products, arithmetic and copies ran while one was open for 9% -> 0% of each run, Pallas kernels for 0% -> 0%
where the time goes in v1:
time: 110 us
  Pallas kernels  92.5 us (84%)
  local copies, waits for them, and re-layouts  16.5 us (15%)
    pallas_call x1, Pallas kernels, on_device(): pl.pallas_call(functools.partial(kernel, scale, depth_total * scale), out...  92.5 us
    reshape x3, local copies, waits for them, and re-layouts, on_device(): conv1_weight.reshape(C, 9, 3, C).transpose(2, 3, 1, 0).reshape(3 * C, 9 * C)  5.97 us
    reshape x4, local copies, waits for them, and re-layouts, on_device(): conv2_weight.reshape(C, 9, 3, C).transpose(2, 3, 1, 0).reshape(3 * C, 9 * C)  4.09 us

profile of v1, /device:TPU:1, one launch (start us, length us, event | category | flops | bytes accessed | tf_op | source)
XLA Modules:
  0.0 110.2 jit_solution(62213880432905152)
XLA Ops:
  0.7 0.0 copy-start.5
  0.7 1.6 %copy.44 = bf16[96,9,3,96]{3,2,0,1:T(4,128)(2,1)S(1)} copy(bf16[96,9,3,96]{3,0,2,1:T(8,128)(2,1)} %bitcast.42) | data formatting | bytes 995328 | tf_op jit(solution)/shard_map/reshape | solution.py:523
  2.3 0.6 reshape.60
  2.9 0.3 copy.32.w2_ref
  3.2 0.0 copy-done.5
  3.2 0.0 copy-start.8
  3.2 0.0 copy-start.9
  3.2 0.0 copy-start.10
  3.3 0.0 copy-start.11
  3.3 0.0 copy-start.7
  3.3 1.6 %copy.29 = bf16[96,9,3,96]{0,2,3,1:T(4,128)(2,1)S(1)} copy(bf16[96,9,3,96]{3,0,2,1:T(8,128)(2,1)S(1)} %bitcast.43) | data formatting | bytes 995328 | tf_op jit(solution)/shard_map/reshape | solution.py:523
  4.9 0.0 copy-start.6
  4.9 0.6 reshape.61
  5.5 0.3 copy.33.w2t_ref
  5.8 0.0 copy-done.8
  5.8 0.0 copy-done.9
  5.8 0.0 copy-done.10
  5.8 0.0 copy-done.11
  5.8 0.1 concatenate.9
  6.0 0.1 copy.30
  6.1 0.0 copy-done.7
  6.1 0.1 pad_maximum_fusion.spread_ref
  6.2 0.0 copy-done.6
  6.2 1.4 %copy.45 = bf16[96,9,3,96]{3,2,0,1:T(4,128)(2,1)} copy(bf16[96,9,3,96]{3,0,2,1:T(8,128)(2,1)S(1)} %bitcast.44) | data formatting | bytes 995328 | tf_op jit(solution)/shard_map/reshape | solution.py:522
  7.6 0.0 copy-start
  7.6 0.0 copy-start.2
  7.6 0.0 copy-start.3
  7.6 0.0 copy-start.4
  7.6 3.2 %reshape.58 = bf16[288,864]{0,1:T(8,128)(2,1)} reshape(bf16[3,96,9,96]{1,0,3,2:T(4,128)(2,1)} %bitcast.41) | data formatting | bytes 995328 | tf_op jit(solution)/shard_map/reshape | solution.py:522
  10.8 1.4 %copy.31.w1_ref = bf16[288,864]{1,0:T(8,128)(2,1)S(1)} copy(bf16[288,864]{0,1:T(8,128)(2,1)} %reshape.58) | data formatting | bytes 995328 | tf_op jit(solution)/shard_map/reshape | solution.py:522
  12.2 0.9 copy.26
  13.1 0.0 copy-done
  13.1 0.0 copy-done.2
  13.2 0.0 copy-done.3
  13.2 0.0 copy-done.4
  13.2 0.0 copy-start.12
  13.2 92.5 %shard_map.149 = (f32[2,8,4,8,128]{4,3,2,1,0:T(8,128)S(1)}, f32[16,128]{1,0:T(8,128)S(1)}) custom-call(bf16[4,96,128]{2,1,0:T(8,128)(2,1)S(1)} %bitcast.34, bf16[288,864]{1,0:T(8,128)(2,1)S(1)} %copy.31.w1_ref, bf16[288,864]{1,0:T(8,128)(2,1)S(1)} %copy.32.w2_ref, bf16[288,864]{1,0:T(8,128)(2,1)S(1)} %copy.33.w2t_ref, bf16[16,96]{1,0:T(8,128)(2,1)S(1)} %bitcast.35, ...), custom_call_target="tpu_custom_call" | custom-call | tf_op jit(solution)/shard_map/pallas_call | solution.py:569
  105.7 0.0 copy-start.1
  105.7 0.7 copy-done.1
  106.4 1.0 reshape.65
  107.5 0.1 constant_dynamic-slice_fusion.2
  107.6 0.1 reshape.67
  107.8 0.1 reshape.68
  107.9 0.7 constant_dynamic-slice_fusion.1
  108.6 0.1 slice_reduce_fusion
  108.7 0.1 div.17
  108.8 0.1 copy.36
  108.9 0.0 copy-done.12
  108.9 0.6 gather_fusion
  109.4 0.1 copy.37
  109.5 0.1 reshape.69
  109.6 0.6 copy.38
  (10 shorter events, 0.1 us)
Async XLA Ops:
  0.7 2.5 %copy-start.5 = (bf16[96,27,96]{2,0,1:T(8,128)(2,1)S(1)}, bf16[96,27,96]{2,0,1:T(8,128)(2,1)}, u32[]{:S(2)}) copy-start(bf16[96,27,96]{2,0,1:T(8,128)(2,1)} %param.16) | copy-start | bytes 1492996
  3.2 2.6 %copy-start.8 = (bf16[96,4]{0,1:T(4,128)(2,1)S(1)}, bf16[96,4]{0,1:T(4,128)(2,1)}, u32[]{:S(2)}) copy-start(bf16[96,4]{0,1:T(4,128)(2,1)} %param.18) | copy-start | bytes 2308
  3.2 2.6 %copy-start.9 = (bf16[96,2]{0,1:T(2,128)(2,1)S(1)}, bf16[96,2]{0,1:T(2,128)(2,1)}, u32[]{:S(2)}) copy-start(bf16[96,2]{0,1:T(2,128)(2,1)} %param.17) | copy-start | bytes 1156
  3.2 2.6 %copy-start.10 = (bf16[96]{0:T(256)(128)(2,1)S(1)}, bf16[96]{0:T(256)(128)(2,1)}, u32[]{:S(2)}) copy-start(bf16[96]{0:T(256)(128)(2,1)} %param.19) | copy-start | bytes 580
  3.3 2.6 %copy-start.11 = (bf16[96,2]{0,1:T(2,128)(2,1)S(1)}, bf16[96,2]{0,1:T(2,128)(2,1)}, u32[]{:S(2)}) copy-start(bf16[96,2]{0,1:T(2,128)(2,1)} %param.20) | copy-start | bytes 1156
  3.3 2.8 %copy-start.7 = (bf16[3,16]{1,0:T(4,128)(2,1)S(1)}, bf16[3,16]{1,0:T(4,128)(2,1)}, u32[]{:S(2)}) copy-start(bf16[3,16]{1,0:T(4,128)(2,1)} %constant.70.clone) | copy-start | bytes 292
  4.9 1.4 %copy-start.6 = (bf16[96,27,96]{2,0,1:T(8,128)(2,1)S(1)}, bf16[96,27,96]{2,0,1:T(8,128)(2,1)}, u32[]{:S(2)}) copy-start(bf16[96,27,96]{2,0,1:T(8,128)(2,1)} %param.15) | copy-start | bytes 1492996
  7.6 5.5 %copy-start = (bf16[2,512,864]{2,1,0:T(8,128)(2,1)S(1)}, bf16[2,512,864]{2,1,0:T(8,128)(2,1)}, u32[]{:S(2)}) copy-start(bf16[2,512,864]{2,1,0:T(8,128)(2,1)} %constant.71.clone.order_ref) | copy-start | bytes 5308420
  7.6 5.5 %copy-start.2 = (s32[2,2,128]{2,1,0:T(2,128)S(1)}, s32[2,2,128]{2,1,0:T(2,128)}, u32[]{:S(2)}) copy-start(s32[2,2,128]{2,1,0:T(2,128)} %param.21) | copy-start | bytes 6148
  7.6 5.5 %copy-start.3 = (s32[2,2,128]{2,1,0:T(2,128)S(1)}, s32[2,2,128]{2,1,0:T(2,128)}, u32[]{:S(2)}) copy-start(s32[2,2,128]{2,1,0:T(2,128)} %param.22) | copy-start | bytes 6148
  7.6 5.5 %copy-start.4 = (s32[2,128]{1,0:T(2,128)S(1)}, s32[2,128]{1,0:T(2,128)}, u32[]{:S(2)}) copy-start(s32[2,128]{1,0:T(2,128)} %param.23) | copy-start | bytes 3076
  13.2 95.7 %copy-start.12 = (s32[9]{0:T(128)S(1)}, s32[9]{0:T(128)}, u32[]{:S(2)}) copy-start(s32[9]{0:T(128)} %constant.79) | copy-start | bytes 112
  105.7 0.7 copy-start.1

commit v2 on v1

--- a/solution.py
+++ b/solution.py
@@ -93,17 +93,21 @@
     scale,
     depth_scale,
     feat_ref,
-    w1_ref,
-    w2_ref,
-    w2t_ref,
+    w1_hbm,
+    w2_hbm,
     heads_ref,
-    spread_ref,
-    order_ref,
+    order_hbm,
     fault_ref,
     horizon_ref,
     salt_ref,
     out_ref,
     gram_ref,
+    raw_w,
+    order_ref,
+    w1_ref,
+    w2_ref,
+    w2t_ref,
+    spread_ref,
     fpad,
     f91,
     f92,
@@ -121,17 +125,20 @@
     o32,
     s1src,
     s1recv,
+    s2sum,
     s2src,
     s2recv,
     r16,
+    s3sum,
     s3src,
     s3recv,
     tbuf,
     pool_x,
-    pool_mine,
-    pool_z,
+    pool_y,
     gram_x,
     gram_z,
+    gram_y,
+    lsem,
     ssem,
     rsem,
 ):
@@ -139,8 +146,6 @@
     inline = zh * 2 + core
     tile = zl * 16 + y * 4 + x
     z = zh * 2 + zl
-    xy = y * 4 + x
-    zc = z * 2 + core
     yhi, ylo = y // 2, y % 2
     p = ylo * 4 + x
 
@@ -170,28 +175,62 @@
     around = [(dx, dz) for dx in (-1, 0, 1) for dz in (-1, 0, 1) if (dx, dz) != (0, 0)]
     halo_to = {d: at_grid(*d) for d in around}
 
-    def plane(k):
-        q = (xy + k) % 16
-        return (zh, core, zl, q // 4, q % 4)
-
-    def column(k):
-        q = (zc + k) % 16
-        return (q // 4, q % 2, (q // 2) % 2, y, x)
-
     partner = (zh, 1 - core, zl, y, x)
 
-    for li in range(2):
-        s3src[li] = jnp.zeros(s3src.shape[1:], F32)
-    dsh[864:896, :] = jnp.zeros((32, 1024), BF16)
+    def at_x(k):
+        return (zh, core, zl, y, (x + k) % 4)
+
+    def at_y(k):
+        return (zh, core, zl, (y + k) % 4, x)
+
+    def at_z(k):
+        q = (z + k) % 8
+        return (q // 2, core, q % 2, y, x)
+
+    def at_eight(k):
+        q = (p + k) % 8
+        return (zh, core, zl, yhi * 2 + q // 4, q % 4)
+
+    def at_depth(k):
+        q = (zl * 2 + yhi + k) % 4
+        return (zh, core, q // 2, (q % 2) * 2 + ylo, x)
+
+    def at_unit(k):
+        q = (core * 2 + yhi + k) % 4
+        return (zh, q // 2, zl, (q % 2) * 2 + ylo, x)
+
+    loads = [
+        pltpu.make_async_copy(src, dst, lsem.at[n])
+        for n, (src, dst) in enumerate(
+            ((w1_hbm, raw_w.at[0]), (w2_hbm, raw_w.at[1]), (order_hbm, order_ref))
+        )
+    ]
+    for load in loads:
+        load.start()
+
+    barrier = pltpu.get_barrier_semaphore()
+    greeted = [halo_to[d] for d in around]
+    greeted += [at_eight(k) for k in range(1, 8)] + [at_z(k) for k in range(1, 8)]
+    greeted += [at_y(k) for k in range(1, 4)]
+    greeted += [at_depth(k) for k in range(1, 4)] + [at_unit(k) for k in range(1, 4)]
+    for device in greeted:
+        pl.semaphore_signal(barrier, inc=1, device_id=device, device_id_type=MESH)
 
     for cell in range(4):
         fpad[(cell // 2 + 1) * 4 + cell % 2 + 1] = feat_ref[cell]
-
-    barrier = pltpu.get_barrier_semaphore()
-    greeted = [halo_to[d] for d in around] + [plane(k) for k in range(1, 16)]
-    greeted += [column(k) for k in range(1, 16)]
-    for device in greeted:
-        pl.semaphore_signal(barrier, inc=1, device_id=device, device_id_type=MESH)
+    for li in range(2):
+        s3sum[li] = jnp.zeros(s3sum.shape[1:], F32)
+    dsh[864:896, :] = jnp.zeros((32, 1024), BF16)
+
+    eye = (
+        lax.broadcasted_iota(jnp.int32, (C, C), 0) == lax.broadcasted_iota(jnp.int32, (C, C), 1)
+    ).astype(BF16)
+
+    def transposed_weight(n, out):
+        for c in range(3):
+            rows = jnp.concatenate([raw_w[n, ab * 3 + c] for ab in range(9)], axis=0)
+            out[c * C : (c + 1) * C, :] = dot_t(eye, rows).astype(BF16)
+
     pl.semaphore_wait(barrier, len(greeted))
 
     copies = []
@@ -201,6 +240,8 @@
                 src = (cx + 1) * 4 + cz + 1
                 dst = (cx - 2 * dx + 1) * 4 + (cz - 2 * dz + 1)
                 copies.append(send(fpad.at[src], fpad.at[dst], halo_to[dx, dz]))
+    loads[0].wait()
+    transposed_weight(0, w1_ref)
     for copy in copies:
         copy.wait_recv()
 
@@ -253,6 +294,40 @@
             made.append(send(buffer.at[4], buffer.at[slot], halo_to[dx, dz]))
         return made
 
+    zs = 2 * core - 1
+    zrow = (zs + 1) * 3
+
+    def blocks_sent(buffer):
+        own = buffer.at[4]
+        far = send(own, buffer.at[(1 - zs) * 3 + 1], at_grid(zs, 0))
+        up = send(own, buffer.at[3], halo_to[0, 1])
+        down = send(own, buffer.at[5], halo_to[0, -1])
+        near = send(own, buffer.at[zrow + 1], partner)
+        return far, up, down, near
+
+    def blocks_passed_on(buffer, first):
+        far, up, down, near = first
+        far.wait_recv()
+        passed = [
+            send(buffer.at[zrow + 1], buffer.at[zrow], halo_to[0, 1]),
+            send(buffer.at[zrow + 1], buffer.at[zrow + 2], halo_to[0, -1]),
+        ]
+        up.wait_recv()
+        passed.append(send(buffer.at[3], buffer.at[zrow], partner))
+        down.wait_recv()
+        passed.append(send(buffer.at[5], buffer.at[zrow + 2], partner))
+        return near, passed
+
+    def blocks_arrived(buffer, second):
+        near, passed = second
+        near.wait_recv()
+        for copy in passed:
+            copy.wait_recv()
+        for copy in passed:
+            copy.wait_send()
+        sent[:] = [copy for copy in sent if not any(copy is done for done in passed)]
+        clear_outside(buffer)
+
     def clear_outside(buffer):
         zeros = jnp.zeros(buffer.shape[1:], buffer.dtype)
 
@@ -281,11 +356,24 @@
         fsend[li] = dot(order_ref[1 - core], field).astype(BF16)
         return send(fsend.at[li], amat.at[li, :, V : 2 * V], partner)
 
-    copies = blocks_around(f92)
+    blocks = blocks_sent(f92)
+    loads[2].wait()
     row_copy = [rows_exchanged(0, f91[...])]
-    for copy in copies:
-        copy.wait_recv()
-    clear_outside(f92)
+    blocks = blocks_passed_on(f92, blocks)
+    loads[1].wait()
+    transposed_weight(1, w2_ref)
+    for c in range(3):
+        for ab in range(9):
+            w2t_ref[c * C : (c + 1) * C, ab * C : (ab + 1) * C] = raw_w[1, ab * 3 + c]
+    heads = heads_ref[...]
+    lane = lax.broadcasted_iota(jnp.int32, (C, 16), 1)
+    of_task = ((lane >= 0) & (lane < 2), (lane >= 2) & (lane < 6), (lane >= 6) & (lane < 9))
+    spread = [jnp.where(of, heads.astype(F32), 0.0) for of in of_task]
+    spread = jnp.concatenate(spread, axis=0).astype(BF16)
+    again = lax.broadcasted_iota(jnp.int32, (16, 48), 1) % 16
+    again = (again == lax.broadcasted_iota(jnp.int32, (16, 48), 0)).astype(BF16)
+    spread_ref[...] = dot(spread, again).astype(BF16)
+    blocks_arrived(f92, blocks)
 
     field9 = f92[...].reshape(9 * C, V)
     pbuf[...] = dot(w2_ref[...], field9)
@@ -294,9 +382,8 @@
     second = (f92[4].astype(F32) + pre * sig).astype(BF16)
     slope2 = sig * (1.0 + pre * (1.0 - sig))
     slope9[4] = slope2.astype(BF16)
-    slope_copies = blocks_around(slope9)
-
-    raw = dot(heads_ref[...], second)
+
+    raw = lax.dot_general(heads, second, (((0,), (0,)), ((), ())), preferred_element_type=F32)
     rows = [raw[n : n + 1, :] for n in range(9)]
     expo = jnp.exp(capped(rows[6]))
 
@@ -307,23 +394,32 @@
 
     zero_row = jnp.zeros((1, 256), F32)
     partial = [depth_sum(expo), depth_sum(expo * rows[7]), depth_sum(expo * rows[8])]
-    pool_x[xy] = jnp.concatenate(partial + [zero_row] * 5, axis=0)
-    copies = [send(pool_x.at[xy], pool_x.at[xy], plane(k)) for k in range(1, 16)]
-    logits = head_logits(rows[0:2], fault_ref[...], scale)
-    logits += head_logits(rows[2:6], horizon_ref[...], scale)
+    pool_x[p] = jnp.concatenate(partial + [zero_row] * 5, axis=0)
+    copies = [send(pool_x.at[p], pool_x.at[p], at_eight(k)) for k in range(1, 8)]
+    blocks = blocks_sent(slope9)
+    fault = jnp.concatenate([fault_ref[a, b : b + 1, :] for a in (0, 1) for b in (0, 1)], axis=1)
+    horizon = jnp.concatenate(
+        [horizon_ref[a, b : b + 1, :] for a in (0, 1) for b in (0, 1)], axis=1
+    )
+    salt = jnp.concatenate([salt_ref[0:1, :], salt_ref[1:2, :]], axis=1)
+    logits = head_logits(rows[0:2], fault, scale)
+    logits += head_logits(rows[2:6], horizon, scale)
+    for copy in copies:
+        copy.wait_recv()
+    pooled = pool_x[0]
+    for j in range(1, 8):
+        pooled = pooled + pool_x[j]
+    quarter = zl * 2 + yhi
+    pool_y[quarter] = pooled
+    copies = [send(pool_y.at[quarter], pool_y.at[quarter], at_depth(k)) for k in range(1, 4)]
+    blocks = blocks_passed_on(slope9, blocks)
     row_copy.append(rows_exchanged(1, field9))
     for copy in copies:
         copy.wait_recv()
-    pooled = pool_x[0]
-    for j in range(1, 16):
-        pooled = pooled + pool_x[j]
-    pool_mine[...] = pooled
-    copy = send(pool_mine, pool_z, (zh, core, 1 - zl, y, x))
-    copy.wait_recv()
-    pooled = pool_mine[...] + pool_z[...]
+    pooled = (pool_y[0] + pool_y[1]) + (pool_y[2] + pool_y[3])
     total = pooled[0:1, :]
     salt_raw = [pooled[1:2, :] / total, pooled[2:3, :] / total]
-    salt_log = head_logits(salt_raw, salt_ref[...], depth_scale)
+    salt_log = head_logits(salt_raw, salt, depth_scale)
     inner = salt_log[0] * salt_raw[0] + salt_log[1] * salt_raw[1]
 
     def per_cell(r):
@@ -357,18 +453,13 @@
             dsh[t * 256 + 192 : t * 256 + 256, cols] = high[0:64, :]
             dsh[768 + 32 * t : 800 + 32 * t, cols] = high[64:96, :]
 
-    def at_x(k):
-        return (zh, core, zl, y, (x + k) % 4)
-
-    def at_y(k):
-        return (zh, core, zl, (y + k) % 4, x)
-
     first_at, first_of = (at_x, at_y), (x, y)
     second_at, second_of = (at_y, at_x), (y, x)
 
-    def stage1(li, d, delta_copy):
+    def stage1(li, d, delta_copies):
         shifted_deltas(draw.at[li], 0, d)
-        delta_copy.wait_recv()
+        for copy in delta_copies:
+            copy.wait_recv()
         shifted_deltas(dpart.at[li], V, d)
         row_copy[li].wait_recv()
         made = []
@@ -392,7 +483,8 @@
             part = o32[li, pl.ds(mine, 64), :]
             for k in range(3):
                 part = part + s1recv[li, h, k].astype(F32)
-            s2src[li, h] = part
+            s2sum[li, h] = part
+            s2src[li, h] = part.astype(BF16)
             for k in range(1, 4):
                 to = pl.multiple_of(((second_of[h] + k) % 4) * 16, 16)
                 src = s2src.at[li, h, pl.ds(to, 16), :]
@@ -404,36 +496,37 @@
             copy.wait_recv()
         for h in range(2):
             mine = pl.multiple_of(second_of[h] * 16, 16)
-            part = s2src[li, h, pl.ds(mine, 16), :]
+            part = s2sum[li, h, pl.ds(mine, 16), :]
             for k in range(3):
-                part = part + s2recv[li, h, k]
+                part = part + s2recv[li, h, k].astype(F32)
             r16[...] = part
             for zz in range(8):
                 for r in range(2):
                     row = zz * 2 + r
                     for lane in range(7):
-                        s3src[li, zz, h * 2 + r, lane : lane + 1, :] = r16[
+                        at = (h * 2 + r) * 8 + lane
+                        s3sum[li, zz, at : at + 1, :] = r16[
                             row : row + 1, lane * 128 : (lane + 1) * 128
                         ]
+        s3src[li] = s3sum[li].astype(BF16)
         made = []
         for k in range(1, 8):
-            q = (z + k) % 8
-            made.append(send(s3src.at[li, q], s3recv.at[li, k - 1], (q // 2, core, q % 2, y, x)))
+            made.append(send(s3src.at[li, (z + k) % 8], s3recv.at[li, k - 1], at_z(k)))
         return made
 
     def stage4(li, copies):
         for copy in copies:
             copy.wait_recv()
-        part = s3src[li, z]
+        part = s3sum[li, z]
         for k in range(7):
-            part = part + s3recv[li, k]
-        tbuf[li, p] = part
-        made = []
-        for k in range(1, 8):
-            q = (p + k) % 8
-            device = (zh, core, zl, yhi * 2 + q // 4, q % 4)
-            made.append(send(tbuf.at[li, p], tbuf.at[li, p], device))
-        return part, made
+            part = part + s3recv[li, k].astype(F32)
+        part = part.reshape(4, 8, 128)
+        tbuf[li, pl.ds(p * 4, 4)] = part
+        return gram_rows(part)
+
+    def shares_spread(li):
+        mine = tbuf.at[li, pl.ds(p * 4, 4)]
+        return [send(mine, mine, at_eight(k)) for k in range(1, 8)]
 
     def gram_rows(part):
         lane = lax.broadcasted_iota(jnp.int32, (4, 128), 1)
@@ -443,19 +536,46 @@
             rest = tail if t == 0 else pltpu.roll(tail, 128 - 32 * t, 1)
             rest = jnp.where(lane < 32, rest, 0.0)
             values.append((part[:, 2 * t, :], part[:, 2 * t + 1, :], rest))
-        found = []
+        found = {}
         for t in range(3):
             for u in range(t, 3):
                 prod = sum(a * b for a, b in zip(values[t], values[u]))
-                found.append(jnp.sum(prod, axis=0, keepdims=True))
+                found[t, u] = found[u, t] = jnp.sum(prod, axis=0, keepdims=True)
         return found
 
+    def own_entries():
+        start = (27 * p) // 8
+        lane = lax.broadcasted_iota(jnp.int32, (6, 128), 1)
+        flat = [jnp.zeros((6, 128), F32) for _ in range(13)]
+        for j in range(5):
+            row = [tbuf[li, start + j] for li in range(2)]
+            pick = lambda s: jnp.concatenate([row[li][s(t)] for li in range(2) for t in range(3)])
+            tail = jnp.concatenate(
+                [
+                    (row[li][6:7] if t == 0 else pltpu.roll(row[li][6:7], 128 - 32 * t, 1))
+                    for li in range(2)
+                    for t in range(3)
+                ]
+            )
+            tiles = [
+                pick(lambda t: slice(2 * t, 2 * t + 1)),
+                pick(lambda t: slice(2 * t + 1, 2 * t + 2)),
+                jnp.where(lane < 32, tail, 0.0),
+            ]
+            at, turn = divmod(288 * j, 128)
+            for n, tile in enumerate(tiles):
+                moved = tile if turn == 0 else pltpu.roll(tile, turn, 1)
+                flat[at + n] += jnp.where(lane >= turn, moved, 0.0)
+                if turn:
+                    flat[at + n + 1] += jnp.where(lane < turn, moved, 0.0)
+        width = 13 * 128
+        flat = jnp.concatenate(flat, axis=1)
+        return pltpu.roll(flat, (width - 36 * ((27 * p) % 8)) % width, 1)
+
     copy = send(draw.at[1], dpart.at[1], partner)
-    reduce2 = stage1(1, D2, copy)
-
-    for copy in slope_copies:
-        copy.wait_recv()
-    clear_outside(slope9)
+    reduce2 = stage1(1, D2, [copy])
+
+    blocks_arrived(slope9, blocks)
     for copy in g_copies:
         copy.wait_recv()
     for s in range(9):
@@ -467,38 +587,56 @@
             d9[t, (8 - s) * C : (9 - s) * C, :] = (cot[t * C : (t + 1) * C, :] * slope).astype(
                 BF16
             )
+    copies = []
     for t in range(3):
         pbuf[...] = dot(w2t_ref[...], d9[t])
         cot = cotc[t * C : (t + 1) * C, :] + taps_added(pbuf, -D2)
         draw[0, t * C : (t + 1) * C, :] = (cot * slope1[...]).astype(BF16)
-    copy = send(draw.at[0], dpart.at[0], partner)
+        part = pl.ds(t * C, C)
+        copies.append(send(draw.at[0, part, :], dpart.at[0, part, :], partner))
     reduce2 = stage2(1, reduce2)
-    reduce1 = stage1(0, D1, copy)
+    reduce1 = stage1(0, D1, copies)
     reduce2 = stage3(1, reduce2)
     reduce1 = stage2(0, reduce1)
-    part2, spread2 = stage4(1, reduce2)
-    found2 = gram_rows(part2)
+    found2 = stage4(1, reduce2)
+    spread = shares_spread(1)
     reduce1 = stage3(0, reduce1)
-    part1, spread1 = stage4(0, reduce1)
-    found = gram_rows(part1) + found2 + [jnp.zeros((4, 128), F32)]
-    gram_x[xy] = jnp.concatenate(found, axis=0)
-    copies = [send(gram_x.at[xy], gram_x.at[xy], plane(k)) for k in range(1, 16)]
+    found = (stage4(0, reduce1), found2)
+    blank = jnp.zeros((2, 128), F32)
+    lane = lax.broadcasted_iota(jnp.int32, (8, 128), 1)
+    part = jnp.zeros((8, 128), F32)
+    for u in range(3):
+        rows = [found[li][t, u] for li in range(2) for t in range(3)] + [blank]
+        column = jnp.sum(jnp.concatenate(rows, axis=0), axis=1, keepdims=True)
+        part = jnp.where(lane == u, column, part)
+    gram_x[p] = part
+    copies = [send(gram_x.at[p], gram_x.at[p], at_eight(k)) for k in range(1, 8)]
+    spread += shares_spread(0)
     for copy in copies:
         copy.wait_recv()
     part = gram_x[0]
-    for j in range(1, 16):
+    for j in range(1, 8):
         part = part + gram_x[j]
-    gram_z[zc] = part
-    copies = [send(gram_z.at[zc], gram_z.at[zc], column(k)) for k in range(1, 16)]
-    for copy in spread2 + spread1:
+    gram_z[z] = part
+    copies = [send(gram_z.at[z], gram_z.at[z], at_z(k)) for k in range(1, 8)]
+    for copy in spread:
         copy.wait_recv()
-    out_ref[...] = tbuf[...]
+    entries = own_entries()
+    for li in range(2):
+        out_ref[li] = entries[3 * li : 3 * li + 3, 0 : out_ref.shape[2]]
     for copy in copies:
         copy.wait_recv()
     part = gram_z[0]
-    for j in range(1, 16):
+    for j in range(1, 8):
         part = part + gram_z[j]
-    gram_ref[...] = part
+    unit = core * 2 + yhi
+    gram_y[unit] = part
+    copies = [send(gram_y.at[unit], gram_y.at[unit], at_unit(k)) for k in range(1, 4)]
+    for copy in copies:
+        copy.wait_recv()
+    part = ((gram_y[0] + gram_y[1]) + (gram_y[2] + gram_y[3])) / NORM
+    for li in range(2):
+        gram_ref[li] = part[3 * li : 3 * li + 3, 0:3]
     for copy in sent:
         copy.wait_send()
 
@@ -519,21 +657,21 @@
     depth_total = depth_cells * lax.axis_size(TILE)
     scale = 1.0 / math.sqrt(inline_cells * lax.axis_size(INLINE) * depth_total * cross_cells)
     cells = features.transpose(1, 2, 0, 3).reshape(4, C, 128)
-    w1 = conv1_weight.reshape(C, 9, 3, C).transpose(2, 3, 1, 0).reshape(3 * C, 9 * C)
-    w2 = conv2_weight.reshape(C, 9, 3, C).transpose(2, 3, 1, 0).reshape(3 * C, 9 * C)
-    w2t = conv2_weight.reshape(C, 9, 3, C).transpose(2, 0, 1, 3).reshape(3 * C, 9 * C)
+    w1 = conv1_weight.transpose(1, 0, 2)
+    w2 = conv2_weight.transpose(1, 0, 2)
+    blank = jnp.zeros((C, 7), BF16)
     heads = jnp.concatenate(
-        [fault_head, horizon_head, salt_query[:, None], salt_head, jnp.zeros((C, 7), BF16)], axis=1
+        [fault_head, horizon_head, salt_query[:, None], salt_head, blank], axis=1
     )
-    task = np.zeros((3, 16), np.float32)
-    task[0, 0:2] = 1.0
-    task[1, 2:6] = 1.0
-    task[2, 6:9] = 1.0
-    spread = (heads[None] * jnp.asarray(task, BF16)[:, None, :]).reshape(3 * C, 16)
-    spread = jnp.concatenate([spread] * 3, axis=1)
     order = jnp.asarray(row_order(), BF16)
 
     scratch = [
+        pltpu.VMEM((2, 27, C, C), BF16),
+        pltpu.VMEM((2, HALF, 9 * C), BF16),
+        pltpu.VMEM((3 * C, 9 * C), BF16),
+        pltpu.VMEM((3 * C, 9 * C), BF16),
+        pltpu.VMEM((3 * C, 9 * C), BF16),
+        pltpu.VMEM((3 * C, 48), BF16),
         pltpu.VMEM((16, C, 128), BF16),
         pltpu.VMEM((9 * C, V), BF16),
         pltpu.VMEM((9, C, V), BF16),
@@ -552,54 +690,37 @@
         pltpu.VMEM((2, HALF, LANES), BF16),
         pltpu.VMEM((2, 2, 3, 64, LANES), BF16),
         pltpu.VMEM((2, 2, 64, LANES), F32),
-        pltpu.VMEM((2, 2, 3, 16, LANES), F32),
+        pltpu.VMEM((2, 2, 64, LANES), BF16),
+        pltpu.VMEM((2, 2, 3, 16, LANES), BF16),
         pltpu.VMEM((16, LANES), F32),
-        pltpu.VMEM((2, 8, 4, 8, 128), F32),
-        pltpu.VMEM((2, 7, 4, 8, 128), F32),
-        pltpu.VMEM((2, 8, 4, 8, 128), F32),
-        pltpu.VMEM((16, 8, 256), F32),
-        pltpu.VMEM((8, 256), F32),
-        pltpu.VMEM((8, 256), F32),
-        pltpu.VMEM((16, 16, 128), F32),
-        pltpu.VMEM((16, 16, 128), F32),
-        pltpu.SemaphoreType.DMA((160,)),
-        pltpu.SemaphoreType.DMA((160,)),
+        pltpu.VMEM((2, 8, 32, 128), F32),
+        pltpu.VMEM((2, 8, 32, 128), BF16),
+        pltpu.VMEM((2, 7, 32, 128), BF16),
+        pltpu.VMEM((2, 32, 8, 128), F32),
+        pltpu.VMEM((8, 8, 256), F32),
+        pltpu.VMEM((4, 8, 256), F32),
+        pltpu.VMEM((8, 8, 128), F32),
+        pltpu.VMEM((8, 8, 128), F32),
+        pltpu.VMEM((4, 8, 128), F32),
+        pltpu.SemaphoreType.DMA((3,)),
+        pltpu.SemaphoreType.DMA((136,)),
+        pltpu.SemaphoreType.DMA((136,)),
     ]
     whole = pl.BlockSpec(memory_space=pltpu.VMEM)
-    units, gram_rows = pl.pallas_call(
+    hbm = pl.BlockSpec(memory_space=pl.ANY)
+    return pl.pallas_call(
         functools.partial(kernel, scale, depth_total * scale),
         out_shape=(
-            jax.ShapeDtypeStruct((2, 8, 4, 8, 128), F32),
-            jax.ShapeDtypeStruct((16, 128), F32),
+            jax.ShapeDtypeStruct((2, 3, NORM // 256), F32),
+            jax.ShapeDtypeStruct((2, 3, 3), F32),
         ),
-        in_specs=[whole] * 10,
+        in_specs=[whole, hbm, hbm, whole, hbm, whole, whole, whole],
         out_specs=(whole, whole),
         scratch_shapes=scratch,
         compiler_params=pltpu.CompilerParams(
-            collective_id=0, has_side_effects=True, vmem_limit_bytes=48 * 1024 * 1024
+            collective_id=0, has_side_effects=True, vmem_limit_bytes=60 * 1024 * 1024
         ),
-    )(
-        cells,
-        w1,
-        w2,
-        w2t,
-        heads.T,
-        spread,
-        order,
-        fault_labels.reshape(1, V),
-        horizon_labels.reshape(1, V),
-        salt_labels.reshape(1, 256),
-    )
-    p = (lax.axis_index("tile_1") % 2) * 4 + lax.axis_index("tile_2")
-    start = (27 * p) // 8
-    mine = lax.dynamic_slice_in_dim(units.reshape(2, 32, 1024), start, 5, 1)
-    main = mine[:, :, 0:768].reshape(2, 5, 3, 256)
-    tail = mine[:, :, 768:864].reshape(2, 5, 3, 32)
-    entries = jnp.concatenate([main, tail], axis=3).transpose(0, 2, 1, 3).reshape(2, 3, 5 * 288)
-    grads = lax.dynamic_slice_in_dim(entries, 36 * ((27 * p) % 8), NORM // 256, 2)
-    sums = jnp.sum(gram_rows[0:12, :], axis=1).reshape(2, 6) / NORM
-    gram = sums[:, np.array([0, 1, 2, 1, 3, 4, 2, 4, 5])].reshape(2, 3, 3)
-    return (grads, gram)
+    )(cells, w1, w2, heads, order, fault_labels, horizon_labels, salt_labels)
 
 
 def solution(mesh):

time: 110 us -> 93.4 us (0.85)
  local copies, waits for them, and re-layouts: 16.5 us -> 6.4 us
  Pallas kernels: 92.5 us -> 86.1 us
    reshape x14 -> x0, local copies, waits for them, and re-layouts: 12.3 us -> none  [the longest x3 5.97 us: on_device(): conv1_weight.reshape(C, 9, 3, C).transpose(2, 3, 1, 0).reshape(3 * C, 9 * C)]
    pallas_call x1, Pallas kernels: 92.5 us -> 86.1 us  [on_device(): pl.pallas_call(functools.partial(kernel, scale, depth_total * scale), out...]
    pallas_call x0 -> x2, local copies, waits for them, and re-layouts: none -> 2.65 us  [on_device(): pl.pallas_call(functools.partial(kernel, scale, depth_total * scale), out...]
    concatenate x2, local copies, waits for them, and re-layouts: 0.25 us -> 2.21 us  [on_device(): jnp.concatenate([fault_head, horizon_head, salt_query[:, None], salt_head...]
    unnamed x29 -> x0, local copies, waits for them, and re-layouts: 1.37 us -> none
where the time goes in v2:
time: 93.4 us; the launch traced here: 93.1 us
  Pallas kernels  86.1 us (92%)
  local copies, waits for them, and re-layouts  6.4 us (7%)
    pallas_call x1, Pallas kernels, on_device(): pl.pallas_call(functools.partial(kernel, scale, depth_total * scale), out...  86.1 us
    pallas_call x2, local copies, waits for them, and re-layouts, on_device(): pl.pallas_call(functools.partial(kernel, scale, depth_total * scale), out...  2.65 us
    concatenate x2, local copies, waits for them, and re-layouts, on_device(): jnp.concatenate([fault_head, horizon_head, salt_query[:, None], salt_head...  2.21 us

profile of v2, /device:TPU:1, one launch (start us, length us, event | category | flops | bytes accessed | tf_op | source)
XLA Modules:
  0.0 93.1 jit_solution(9812408538902320762)
XLA Ops:
  0.6 1.5 %concatenate.3 = bf16[96,16]{0,1:T(8,128)(2,1)S(1)} concatenate(bf16[96,2]{0,1:T(2,128)(2,1)} %param.14, bf16[96,4]{0,1:T(4,128)(2,1)} %param.15, bf16[96,1]{0,1:T(2,128)(2,1)} %bitcast.9, bf16[96,2]{0,1:T(2,128)(2,1)} %param.17, bf16[96,7]{0,1:T(8,128)(2,1)S(1)} %broadcast_in_dim.7), dimensions={1} | concatenate | bytes 6144 | tf_op jit(solution)/shard_map/concatenate | solution.py:663
  2.1 0.7 copy.21.heads_ref
  2.8 1.5 %copy.20 = bf16[2,2,96,128]{3,2,1,0:T(8,128)(2,1)} copy(bf16[2,2,96,128]{3,1,0,2:T(2,128)(2,1)} %bitcast.8) | data formatting | bytes 196608 | tf_op jit(solution)/shard_map/transpose | solution.py:659
  4.4 86.1 %shard_map.122 = (f32[2,3,972]{2,1,0:T(4,128)}, f32[2,3,3]{2,1,0:T(4,128)}) custom-call(bf16[4,96,128]{2,1,0:T(8,128)(2,1)} %bitcast.7, bf16[27,96,96]{2,1,0:T(8,128)(2,1)} %bitcast.5, bf16[27,96,96]{2,1,0:T(8,128)(2,1)} %bitcast.6, bf16[96,16]{1,0:T(8,128)(2,1)} %copy.21.heads_ref, bf16[2,512,864]{2,1,0:T(8,128)(2,1)} %constant.4.clone.order_hbm, ...), custom_call_target="tpu_custom_call" | custom-call | tf_op jit(solution)/shard_map/pallas_call | solution.py:711
  90.5 1.4 %copy.22 = f32[2,3,972]{2,0,1:T(2,128)} copy(f32[2,3,972]{2,1,0:T(4,128)} %get-tuple-element.4) | data formatting | bytes 46656 | tf_op jit(solution)/shard_map/pallas_call | solution.py:711
  91.9 1.3 %copy.23 = f32[2,3,3]{2,0,1:T(2,128)} copy(f32[2,3,3]{2,1,0:T(4,128)} %get-tuple-element.5) | data formatting | bytes 144 | tf_op jit(solution)/shard_map/pallas_call | solution.py:711
  (1 shorter events, 0.0 us)

commit v3 on v2

--- a/solution.py
+++ b/solution.py
@@ -82,11 +82,11 @@
 
 
 def three_parts(g):
-    hi = g.astype(BF16)
-    rest = g - hi.astype(F32)
-    mid = rest.astype(BF16)
-    low = (rest - mid.astype(F32)).astype(BF16)
-    return jnp.concatenate([hi, mid, low], axis=0)
+    hi = g.astype(BF16).astype(F32)
+    rest = g - hi
+    mid = rest.astype(BF16).astype(F32)
+    parts = [hi, mid, rest - mid, jnp.zeros(g.shape, F32)]
+    return jnp.concatenate(parts, axis=0).astype(BF16)
 
 
 def kernel(
@@ -95,7 +95,10 @@
     feat_ref,
     w1_hbm,
     w2_hbm,
-    heads_ref,
+    fault_head,
+    horizon_head,
+    query_ref,
+    salt_head,
     order_hbm,
     fault_ref,
     horizon_ref,
@@ -107,12 +110,14 @@
     w1_ref,
     w2_ref,
     w2t_ref,
-    spread_ref,
+    spread_a,
+    spread_b,
     fpad,
     f91,
     f92,
     slope9,
-    g9,
+    g9a,
+    g9b,
     d9,
     slope1,
     cotc,
@@ -205,14 +210,14 @@
             ((w1_hbm, raw_w.at[0]), (w2_hbm, raw_w.at[1]), (order_hbm, order_ref))
         )
     ]
-    for load in loads:
-        load.start()
+    loads[0].start()
 
     barrier = pltpu.get_barrier_semaphore()
     greeted = [halo_to[d] for d in around]
     greeted += [at_eight(k) for k in range(1, 8)] + [at_z(k) for k in range(1, 8)]
-    greeted += [at_y(k) for k in range(1, 4)]
-    greeted += [at_depth(k) for k in range(1, 4)] + [at_unit(k) for k in range(1, 4)]
+    greeted += [at_y(2), (zh, core, zl, 3 - y, x)]
+    across = (1 - yhi) * 2 + ylo
+    greeted += [(zh, core, 1 - zl, across, x), (zh, 1 - core, zl, across, x)]
     for device in greeted:
         pl.semaphore_signal(barrier, inc=1, device_id=device, device_id_type=MESH)
 
@@ -231,6 +236,10 @@
             rows = jnp.concatenate([raw_w[n, ab * 3 + c] for ab in range(9)], axis=0)
             out[c * C : (c + 1) * C, :] = dot_t(eye, rows).astype(BF16)
 
+    loads[0].wait()
+    loads[2].start()
+    loads[1].start()
+    transposed_weight(0, w1_ref)
     pl.semaphore_wait(barrier, len(greeted))
 
     copies = []
@@ -240,8 +249,6 @@
                 src = (cx + 1) * 4 + cz + 1
                 dst = (cx - 2 * dx + 1) * 4 + (cz - 2 * dz + 1)
                 copies.append(send(fpad.at[src], fpad.at[dst], halo_to[dx, dz]))
-    loads[0].wait()
-    transposed_weight(0, w1_ref)
     for copy in copies:
         copy.wait_recv()
 
@@ -365,14 +372,27 @@
     for c in range(3):
         for ab in range(9):
             w2t_ref[c * C : (c + 1) * C, ab * C : (ab + 1) * C] = raw_w[1, ab * 3 + c]
-    heads = heads_ref[...]
+    heads = jnp.concatenate(
+        [
+            fault_head[...].astype(F32),
+            horizon_head[...].astype(F32),
+            jnp.zeros((2, C), F32),
+            query_ref[...].astype(F32),
+            salt_head[...].astype(F32),
+            jnp.zeros((5, C), F32),
+        ],
+        axis=0,
+    ).astype(BF16)
+    column = dot_t(eye, heads)
     lane = lax.broadcasted_iota(jnp.int32, (C, 16), 1)
-    of_task = ((lane >= 0) & (lane < 2), (lane >= 2) & (lane < 6), (lane >= 6) & (lane < 9))
-    spread = [jnp.where(of, heads.astype(F32), 0.0) for of in of_task]
-    spread = jnp.concatenate(spread, axis=0).astype(BF16)
-    again = lax.broadcasted_iota(jnp.int32, (16, 48), 1) % 16
-    again = (again == lax.broadcasted_iota(jnp.int32, (16, 48), 0)).astype(BF16)
-    spread_ref[...] = dot(spread, again).astype(BF16)
+    of_task = [jnp.where(lane < 2, column, 0.0), jnp.where((lane >= 2) & (lane < 6), column, 0.0)]
+    of_task = jnp.concatenate(of_task, axis=0).astype(BF16)
+    row = lax.broadcasted_iota(jnp.int32, (16, 32), 0)
+    again = lax.broadcasted_iota(jnp.int32, (16, 32), 1)
+    again_a = ((row == again % 8) & (again < 24)).astype(BF16)
+    again_b = ((row == again % 8 + 8) & (again < 24)).astype(BF16)
+    spread_a[...] = dot(of_task, again_a).astype(BF16)
+    spread_b[...] = dot(column.astype(BF16), again_b).astype(BF16)
     blocks_arrived(f92, blocks)
 
     field9 = f92[...].reshape(9 * C, V)
@@ -383,9 +403,9 @@
     slope2 = sig * (1.0 + pre * (1.0 - sig))
     slope9[4] = slope2.astype(BF16)
 
-    raw = lax.dot_general(heads, second, (((0,), (0,)), ((), ())), preferred_element_type=F32)
-    rows = [raw[n : n + 1, :] for n in range(9)]
-    expo = jnp.exp(capped(rows[6]))
+    raw = dot(heads, second)
+    rows = [raw[n : n + 1, :] for n in range(11)]
+    expo = jnp.exp(capped(rows[8]))
 
     def depth_sum(r):
         return jnp.concatenate(
@@ -393,7 +413,7 @@
         )
 
     zero_row = jnp.zeros((1, 256), F32)
-    partial = [depth_sum(expo), depth_sum(expo * rows[7]), depth_sum(expo * rows[8])]
+    partial = [depth_sum(expo), depth_sum(expo * rows[9]), depth_sum(expo * rows[10])]
     pool_x[p] = jnp.concatenate(partial + [zero_row] * 5, axis=0)
     copies = [send(pool_x.at[p], pool_x.at[p], at_eight(k)) for k in range(1, 8)]
     blocks = blocks_sent(slope9)
@@ -404,6 +424,25 @@
     salt = jnp.concatenate([salt_ref[0:1, :], salt_ref[1:2, :]], axis=1)
     logits = head_logits(rows[0:2], fault, scale)
     logits += head_logits(rows[2:6], horizon, scale)
+    g = jnp.concatenate(logits + [jnp.zeros((2, V), F32)], axis=0)
+    g9a[4] = g
+    ga_copies = blocks_around(g9a)
+
+    def own_deltas(tasks, cot):
+        for n, t in enumerate(tasks):
+            part = cot[n * C : (n + 1) * C, :]
+            cotc[t * C : (t + 1) * C, :] = part
+            delta = (part * slope2).astype(BF16)
+            d9[t, 4 * C : 5 * C, :] = delta
+            draw[1, t * C : (t + 1) * C, :] = delta
+
+    def deltas_sent(li, tasks):
+        part = pl.ds(tasks[0] * C, len(tasks) * C)
+        return send(draw.at[li, part, :], dpart.at[li, part, :], partner)
+
+    own_deltas((0, 1), dot(spread_a[...], three_parts(g)))
+    delta_copy = deltas_sent(1, (0, 1))
+    row_copy.append(rows_exchanged(1, field9))
     for copy in copies:
         copy.wait_recv()
     pooled = pool_x[0]
@@ -413,36 +452,9 @@
     pool_y[quarter] = pooled
     copies = [send(pool_y.at[quarter], pool_y.at[quarter], at_depth(k)) for k in range(1, 4)]
     blocks = blocks_passed_on(slope9, blocks)
-    row_copy.append(rows_exchanged(1, field9))
-    for copy in copies:
-        copy.wait_recv()
-    pooled = (pool_y[0] + pool_y[1]) + (pool_y[2] + pool_y[3])
-    total = pooled[0:1, :]
-    salt_raw = [pooled[1:2, :] / total, pooled[2:3, :] / total]
-    salt_log = head_logits(salt_raw, salt, depth_scale)
-    inner = salt_log[0] * salt_raw[0] + salt_log[1] * salt_raw[1]
-
-    def per_cell(r):
-        return jnp.concatenate([r[:, 0:128], r[:, 0:128], r[:, 128:256], r[:, 128:256]], axis=1)
-
-    attn = expo / per_cell(total)
-    wide = [per_cell(r) for r in salt_log]
-    along = wide[0] * rows[7] + wide[1] * rows[8]
-    dscore = attn * (along - per_cell(inner)) * cap_slope(rows[6])
-    voxel = logits + [dscore, attn * wide[0], attn * wide[1]]
-    g = jnp.concatenate(voxel + [jnp.zeros((7, V), F32)], axis=0)
-    g9[4] = g
-    g_copies = blocks_around(g9)
-
-    cot = dot(spread_ref[...], three_parts(g))
-    cotc[...] = cot
-    for t in range(3):
-        delta = (cot[t * C : (t + 1) * C, :] * slope2).astype(BF16)
-        d9[t, 4 * C : 5 * C, :] = delta
-        draw[1, t * C : (t + 1) * C, :] = delta
-
-    def shifted_deltas(ref, at, d):
-        for t in range(3):
+
+    def shifted_deltas(ref, at, d, tasks):
+        for t in tasks:
             mid = ref[t * C : (t + 1) * C, :]
             wide = mid.astype(F32)
             low = shifted(wide, d).astype(BF16)
@@ -453,25 +465,50 @@
             dsh[t * 256 + 192 : t * 256 + 256, cols] = high[0:64, :]
             dsh[768 + 32 * t : 800 + 32 * t, cols] = high[64:96, :]
 
+    def products(li, d, tasks, lanes, delta_copy):
+        shifted_deltas(draw.at[li], 0, d, tasks)
+        delta_copy.wait_recv()
+        shifted_deltas(dpart.at[li], V, d, tasks)
+        for h in range(2):
+            part = slice(h * 256, (h + 1) * 256)
+            prod = dot_t(amat[li, part, :], dsh[lanes, :])
+            o32[li, part, lanes] = prod
+            s1src[li, part, lanes] = prod.astype(BF16)
+
+    row_copy[1].wait_recv()
+    products(1, D2, (0, 1), slice(0, 512), delta_copy)
+    for copy in copies:
+        copy.wait_recv()
+    pooled = (pool_y[0] + pool_y[1]) + (pool_y[2] + pool_y[3])
+    total = pooled[0:1, :]
+    salt_raw = [pooled[1:2, :] / total, pooled[2:3, :] / total]
+    salt_log = head_logits(salt_raw, salt, depth_scale)
+    inner = salt_log[0] * salt_raw[0] + salt_log[1] * salt_raw[1]
+
+    def per_cell(r):
+        return jnp.concatenate([r[:, 0:128], r[:, 0:128], r[:, 128:256], r[:, 128:256]], axis=1)
+
+    attn = expo / per_cell(total)
+    wide = [per_cell(r) for r in salt_log]
+    along = wide[0] * rows[9] + wide[1] * rows[10]
+    dscore = attn * (along - per_cell(inner)) * cap_slope(rows[8])
+    voxel = [dscore, attn * wide[0], attn * wide[1]]
+    g = jnp.concatenate(voxel + [jnp.zeros((5, V), F32)], axis=0)
+    g9b[4] = g
+    gb_copies = blocks_around(g9b)
+    own_deltas((2,), dot(spread_b[...], three_parts(g)))
+    delta_copy = deltas_sent(1, (2,))
+
     first_at, first_of = (at_x, at_y), (x, y)
     second_at, second_of = (at_y, at_x), (y, x)
 
-    def stage1(li, d, delta_copies):
-        shifted_deltas(draw.at[li], 0, d)
-        for copy in delta_copies:
-            copy.wait_recv()
-        shifted_deltas(dpart.at[li], V, d)
-        row_copy[li].wait_recv()
+    def stage1(li, lanes):
         made = []
         for h in range(2):
-            part = slice(h * 256, (h + 1) * 256)
-            prod = dot_t(amat[li, part, :], dsh[...])
-            o32[li, part, :] = prod
-            s1src[li, part, :] = prod.astype(BF16)
             for k in range(1, 4):
                 to = h * 256 + ((first_of[h] + k) % 4) * 64
-                src = s1src.at[li, pl.ds(pl.multiple_of(to, 64), 64), :]
-                made.append(send(src, s1recv.at[li, h, k - 1], first_at[h](k)))
+                src = s1src.at[li, pl.ds(pl.multiple_of(to, 64), 64), lanes]
+                made.append(send(src, s1recv.at[li, h, k - 1, :, lanes], first_at[h](k)))
         return made
 
     def stage2(li, copies):
@@ -572,30 +609,38 @@
         flat = jnp.concatenate(flat, axis=1)
         return pltpu.roll(flat, (width - 36 * ((27 * p) % 8)) % width, 1)
 
-    copy = send(draw.at[1], dpart.at[1], partner)
-    reduce2 = stage1(1, D2, [copy])
+    reduce2 = stage1(1, pl.ds(0, 512))
+    products(1, D2, (2,), slice(512, LANES), delta_copy)
+    reduce2 += stage1(1, pl.ds(512, LANES - 512))
+
+    def first_deltas(tasks, spread, g9):
+        for s in range(9):
+            if s == 4:
+                continue
+            cot = dot(spread[...], three_parts(g9[s]))
+            slope = slope9[s].astype(F32)
+            for n, t in enumerate(tasks):
+                delta = (cot[n * C : (n + 1) * C, :] * slope).astype(BF16)
+                d9[t, (8 - s) * C : (9 - s) * C, :] = delta
+        for t in tasks:
+            pbuf[...] = dot(w2t_ref[...], d9[t])
+            cot = cotc[t * C : (t + 1) * C, :] + taps_added(pbuf, -D2)
+            draw[0, t * C : (t + 1) * C, :] = (cot * slope1[...]).astype(BF16)
+        return deltas_sent(0, tasks)
 
     blocks_arrived(slope9, blocks)
-    for copy in g_copies:
+    for copy in ga_copies:
         copy.wait_recv()
-    for s in range(9):
-        if s == 4:
-            continue
-        cot = dot(spread_ref[...], three_parts(g9[s]))
-        slope = slope9[s].astype(F32)
-        for t in range(3):
-            d9[t, (8 - s) * C : (9 - s) * C, :] = (cot[t * C : (t + 1) * C, :] * slope).astype(
-                BF16
-            )
-    copies = []
-    for t in range(3):
-        pbuf[...] = dot(w2t_ref[...], d9[t])
-        cot = cotc[t * C : (t + 1) * C, :] + taps_added(pbuf, -D2)
-        draw[0, t * C : (t + 1) * C, :] = (cot * slope1[...]).astype(BF16)
-        part = pl.ds(t * C, C)
-        copies.append(send(draw.at[0, part, :], dpart.at[0, part, :], partner))
+    delta_copy = first_deltas((0, 1), spread_a, g9a)
+    row_copy[0].wait_recv()
+    products(0, D1, (0, 1), slice(0, 512), delta_copy)
+    reduce1 = stage1(0, pl.ds(0, 512))
+    for copy in gb_copies:
+        copy.wait_recv()
+    delta_copy = first_deltas((2,), spread_b, g9b)
     reduce2 = stage2(1, reduce2)
-    reduce1 = stage1(0, D1, copies)
+    products(0, D1, (2,), slice(512, LANES), delta_copy)
+    reduce1 += stage1(0, pl.ds(512, LANES - 512))
     reduce2 = stage3(1, reduce2)
     reduce1 = stage2(0, reduce1)
     found2 = stage4(1, reduce2)
@@ -623,7 +668,9 @@
         copy.wait_recv()
     entries = own_entries()
     for li in range(2):
-        out_ref[li] = entries[3 * li : 3 * li + 3, 0 : out_ref.shape[2]]
+        for t in range(3):
+            row = 3 * li + t
+            out_ref[t, li : li + 1, :] = entries[row : row + 1, 0 : out_ref.shape[2]]
     for copy in copies:
         copy.wait_recv()
     part = gram_z[0]
@@ -636,7 +683,9 @@
         copy.wait_recv()
     part = ((gram_y[0] + gram_y[1]) + (gram_y[2] + gram_y[3])) / NORM
     for li in range(2):
-        gram_ref[li] = part[3 * li : 3 * li + 3, 0:3]
+        for t in range(3):
+            row = 3 * li + t
+            gram_ref[t, li : li + 1, :] = part[row : row + 1, 0:3]
     for copy in sent:
         copy.wait_send()
 
@@ -659,10 +708,6 @@
     cells = features.transpose(1, 2, 0, 3).reshape(4, C, 128)
     w1 = conv1_weight.transpose(1, 0, 2)
     w2 = conv2_weight.transpose(1, 0, 2)
-    blank = jnp.zeros((C, 7), BF16)
-    heads = jnp.concatenate(
-        [fault_head, horizon_head, salt_query[:, None], salt_head, blank], axis=1
-    )
     order = jnp.asarray(row_order(), BF16)
 
     scratch = [
@@ -671,12 +716,14 @@
         pltpu.VMEM((3 * C, 9 * C), BF16),
         pltpu.VMEM((3 * C, 9 * C), BF16),
         pltpu.VMEM((3 * C, 9 * C), BF16),
-        pltpu.VMEM((3 * C, 48), BF16),
+        pltpu.VMEM((2 * C, 32), BF16),
+        pltpu.VMEM((C, 32), BF16),
         pltpu.VMEM((16, C, 128), BF16),
         pltpu.VMEM((9 * C, V), BF16),
         pltpu.VMEM((9, C, V), BF16),
         pltpu.VMEM((9, C, V), BF16),
-        pltpu.VMEM((9, 16, V), F32),
+        pltpu.VMEM((9, 8, V), F32),
+        pltpu.VMEM((9, 8, V), F32),
         pltpu.VMEM((3, 9 * C, V), BF16),
         pltpu.VMEM((C, V), F32),
         pltpu.VMEM((3 * C, V), F32),
@@ -703,24 +750,37 @@
         pltpu.VMEM((8, 8, 128), F32),
         pltpu.VMEM((4, 8, 128), F32),
         pltpu.SemaphoreType.DMA((3,)),
-        pltpu.SemaphoreType.DMA((136,)),
-        pltpu.SemaphoreType.DMA((136,)),
+        pltpu.SemaphoreType.DMA((160,)),
+        pltpu.SemaphoreType.DMA((160,)),
     ]
     whole = pl.BlockSpec(memory_space=pltpu.VMEM)
     hbm = pl.BlockSpec(memory_space=pl.ANY)
-    return pl.pallas_call(
+    grads, gram = pl.pallas_call(
         functools.partial(kernel, scale, depth_total * scale),
         out_shape=(
-            jax.ShapeDtypeStruct((2, 3, NORM // 256), F32),
-            jax.ShapeDtypeStruct((2, 3, 3), F32),
+            jax.ShapeDtypeStruct((3, 2, NORM // 256), F32),
+            jax.ShapeDtypeStruct((3, 2, 3), F32),
         ),
-        in_specs=[whole, hbm, hbm, whole, hbm, whole, whole, whole],
+        in_specs=[whole, hbm, hbm] + [whole] * 4 + [hbm] + [whole] * 3,
         out_specs=(whole, whole),
         scratch_shapes=scratch,
         compiler_params=pltpu.CompilerParams(
             collective_id=0, has_side_effects=True, vmem_limit_bytes=60 * 1024 * 1024
         ),
-    )(cells, w1, w2, heads, order, fault_labels, horizon_labels, salt_labels)
+    )(
+        cells,
+        w1,
+        w2,
+        fault_head.T,
+        horizon_head.T,
+        salt_query[None],
+        salt_head.T,
+        order,
+        fault_labels,
+        horizon_labels,
+        salt_labels,
+    )
+    return grads.transpose(1, 0, 2), gram.transpose(1, 0, 2)
 
 
 def solution(mesh):

time: 93.4 us -> 86.6 us (0.927)
  Pallas kernels: 86.1 us -> 81.5 us
  local copies, waits for them, and re-layouts: 6.4 us -> 4.15 us
    pallas_call x1, Pallas kernels: 86.1 us -> 81.5 us  [on_device(): pl.pallas_call(functools.partial(kernel, scale, depth_total * scale), out...]
    pallas_call x2 -> x0, local copies, waits for them, and re-layouts: 2.65 us -> none  [on_device(): pl.pallas_call(functools.partial(kernel, scale, depth_total * scale), out...]
    unnamed x0 -> x2, local copies, waits for them, and re-layouts: none -> 2.61 us
    concatenate x2 -> x0, local copies, waits for them, and re-layouts: 2.21 us -> none  [on_device(): jnp.concatenate([fault_head, horizon_head, salt_query[:, None], salt_head...]
where the time goes in v3:
time: 86.6 us; the launch traced here: 86.3 us
  Pallas kernels  81.5 us (94%)
  local copies, waits for them, and re-layouts  4.15 us (5%)
    pallas_call x1, Pallas kernels, on_device(): pl.pallas_call(functools.partial(kernel, scale, depth_total * scale), out...  81.5 us
    unnamed x2, local copies, waits for them, and re-layouts  2.61 us

profile of v3, /device:TPU:1, one launch (start us, length us, event | category | flops | bytes accessed | tf_op | source)
XLA Modules:
  0.0 86.3 jit_solution(6525728398003247481)
XLA Ops:
  0.6 1.5 %copy.13 = bf16[2,2,96,128]{3,2,1,0:T(8,128)(2,1)} copy(bf16[2,2,96,128]{3,1,0,2:T(2,128)(2,1)} %bitcast.13) | data formatting | bytes 196608 | tf_op jit(solution)/shard_map/transpose | solution.py:708
  2.2 81.5 %shard_map.122 = (f32[3,2,972]{2,1,0:T(2,128)}, f32[3,2,3]{2,1,0:T(2,128)}) custom-call(bf16[4,96,128]{2,1,0:T(8,128)(2,1)} %bitcast.12, bf16[27,96,96]{2,1,0:T(8,128)(2,1)} %bitcast.10, bf16[27,96,96]{2,1,0:T(8,128)(2,1)} %bitcast.11, bf16[2,96]{1,0:T(2,128)(2,1)} %bitcast.17, bf16[4,96]{1,0:T(4,128)(2,1)} %bitcast.16, bf16[1,96]{1,0:T(2,128)(2,1)} %bitcast.18, ...), custom_call_target="tpu_custom_call" | custom-call | tf_op jit(solution)/shard_map/pallas_call | solution.py:758
  83.7 1.3 %copy.16 = f32[2,3,972]{2,0,1:T(2,128)} copy(f32[2,3,972]{2,0,1:T(2,128)} %bitcast.14) | data formatting | bytes 46656
  85.0 1.3 %copy.17 = f32[2,3,3]{2,0,1:T(2,128)} copy(f32[2,3,3]{2,0,1:T(2,128)} %bitcast.15) | data formatting | bytes 144

commit v4 on v3

--- a/solution.py
+++ b/solution.py
@@ -469,11 +469,9 @@
         shifted_deltas(draw.at[li], 0, d, tasks)
         delta_copy.wait_recv()
         shifted_deltas(dpart.at[li], V, d, tasks)
-        for h in range(2):
-            part = slice(h * 256, (h + 1) * 256)
-            prod = dot_t(amat[li, part, :], dsh[lanes, :])
-            o32[li, part, lanes] = prod
-            s1src[li, part, lanes] = prod.astype(BF16)
+        prod = dot_t(amat[li], dsh[lanes, :])
+        o32[li, :, lanes] = prod
+        s1src[li, :, lanes] = prod.astype(BF16)
 
     row_copy[1].wait_recv()
     products(1, D2, (0, 1), slice(0, 512), delta_copy)
@@ -561,8 +559,8 @@
         tbuf[li, pl.ds(p * 4, 4)] = part
         return gram_rows(part)
 
-    def shares_spread(li):
-        mine = tbuf.at[li, pl.ds(p * 4, 4)]
+    def shares_spread():
+        mine = tbuf.at[:, pl.ds(p * 4, 4)]
         return [send(mine, mine, at_eight(k)) for k in range(1, 8)]
 
     def gram_rows(part):
@@ -641,11 +639,10 @@
     reduce2 = stage2(1, reduce2)
     products(0, D1, (2,), slice(512, LANES), delta_copy)
     reduce1 += stage1(0, pl.ds(512, LANES - 512))
+    reduce1 = stage2(0, reduce1)
     reduce2 = stage3(1, reduce2)
-    reduce1 = stage2(0, reduce1)
+    reduce1 = stage3(0, reduce1)
     found2 = stage4(1, reduce2)
-    spread = shares_spread(1)
-    reduce1 = stage3(0, reduce1)
     found = (stage4(0, reduce1), found2)
     blank = jnp.zeros((2, 128), F32)
     lane = lax.broadcasted_iota(jnp.int32, (8, 128), 1)
@@ -656,7 +653,7 @@
         part = jnp.where(lane == u, column, part)
     gram_x[p] = part
     copies = [send(gram_x.at[p], gram_x.at[p], at_eight(k)) for k in range(1, 8)]
-    spread += shares_spread(0)
+    spread = shares_spread()
     for copy in copies:
         copy.wait_recv()
     part = gram_x[0]
@@ -755,6 +752,7 @@
     ]
     whole = pl.BlockSpec(memory_space=pltpu.VMEM)
     hbm = pl.BlockSpec(memory_space=pl.ANY)
+    in_hbm = lambda a: pltpu.with_memory_space_constraint(a, pltpu.HBM)
     grads, gram = pl.pallas_call(
         functools.partial(kernel, scale, depth_total * scale),
         out_shape=(
@@ -765,20 +763,20 @@
         out_specs=(whole, whole),
         scratch_shapes=scratch,
         compiler_params=pltpu.CompilerParams(
-            collective_id=0, has_side_effects=True, vmem_limit_bytes=60 * 1024 * 1024
+            collective_id=0, has_side_effects=True, vmem_limit_bytes=50 * 1024 * 1024
         ),
     )(
         cells,
-        w1,
-        w2,
-        fault_head.T,
-        horizon_head.T,
-        salt_query[None],
-        salt_head.T,
-        order,
-        fault_labels,
-        horizon_labels,
-        salt_labels,
+        in_hbm(w1),
+        in_hbm(w2),
+        in_hbm(fault_head.T),
+        in_hbm(horizon_head.T),
+        in_hbm(salt_query[None]),
+        in_hbm(salt_head.T),
+        in_hbm(order),
+        in_hbm(fault_labels),
+        in_hbm(horizon_labels),
+        in_hbm(salt_labels),
     )
     return grads.transpose(1, 0, 2), gram.transpose(1, 0, 2)
 

time: 86.6 us -> 83.2 us (0.961)
  local copies, waits for them, and re-layouts: 4.15 us -> 2.1 us
  Pallas kernels: 81.5 us -> 80.3 us
    unnamed x2, local copies, waits for them, and re-layouts: 2.61 us -> 1.19 us
    pallas_call x1, Pallas kernels: 81.5 us -> 80.3 us  [on_device(): pl.pallas_call(functools.partial(kernel, scale, depth_total * scale), out...]
where the time goes in v4:
time: 83.2 us; the launch traced here: 83 us
  Pallas kernels  80.3 us (97%)
  local copies, waits for them, and re-layouts  2.1 us (3%)
    pallas_call x1, Pallas kernels, on_device(): pl.pallas_call(functools.partial(kernel, scale, depth_total * scale), out...  80.3 us

profile of v4, /device:TPU:1, one launch (start us, length us, event | category | flops | bytes accessed | tf_op | source)
XLA Modules:
  0.0 83.0 jit_solution(2720884690718994629)
XLA Ops:
  0.6 0.9 %copy.13 = bf16[2,2,96,128]{3,2,1,0:T(8,128)(2,1)S(1)} copy(bf16[2,2,96,128]{3,1,0,2:T(2,128)(2,1)} %bitcast.15) | data formatting | bytes 196608 | tf_op jit(solution)/shard_map/transpose | solution.py:705
  1.5 80.3 %shard_map.122 = (f32[3,2,972]{2,1,0:T(2,128)S(1)}, f32[3,2,3]{2,1,0:T(2,128)S(1)}) custom-call(bf16[4,96,128]{2,1,0:T(8,128)(2,1)S(1)} %bitcast.10, bf16[27,96,96]{2,1,0:T(8,128)(2,1)} %bitcast.13, bf16[27,96,96]{2,1,0:T(8,128)(2,1)} %bitcast.14, bf16[2,96]{1,0:T(2,128)(2,1)} %bitcast.17, bf16[4,96]{1,0:T(4,128)(2,1)} %bitcast.16, bf16[1,96]{1,0:T(2,128)(2,1)} %bitcast.18, ...), custom_call_target="tpu_custom_call" | custom-call | tf_op jit(solution)/shard_map/pallas_call | solution.py:756
  81.9 0.6 copy.16
  82.5 0.6 copy.17

commit v5 on v4

--- a/solution.py
+++ b/solution.py
@@ -172,6 +172,12 @@
         sent.append(copy)
         return copy
 
+    def sends_done(keep):
+        old = sent[: len(sent) - keep]
+        for copy in old:
+            copy.wait_send()
+        del sent[: len(old)]
+
     def at_grid(dx, dz):
         i = (inline + dx + 8) % 8
         t = (tile + dz + 32) % 32
@@ -639,6 +645,7 @@
     reduce2 = stage2(1, reduce2)
     products(0, D1, (2,), slice(512, LANES), delta_copy)
     reduce1 += stage1(0, pl.ds(512, LANES - 512))
+    sends_done(25)
     reduce1 = stage2(0, reduce1)
     reduce2 = stage3(1, reduce2)
     reduce1 = stage3(0, reduce1)
@@ -654,6 +661,7 @@
     gram_x[p] = part
     copies = [send(gram_x.at[p], gram_x.at[p], at_eight(k)) for k in range(1, 8)]
     spread = shares_spread()
+    sends_done(14)
     for copy in copies:
         copy.wait_recv()
     part = gram_x[0]
@@ -683,8 +691,7 @@
         for t in range(3):
             row = 3 * li + t
             gram_ref[t, li : li + 1, :] = part[row : row + 1, 0:3]
-    for copy in sent:
-        copy.wait_send()
+    sends_done(0)
 
 
 def on_device(

time: 83.2 us -> 83.1 us (level)
  no operation moved by 1% of the time
where the time goes in v5:
time: 83.1 us; the launch traced here: 82.9 us
  Pallas kernels  80.1 us (96%)
  local copies, waits for them, and re-layouts  2.1 us (3%)
    pallas_call x1, Pallas kernels, on_device(): pl.pallas_call(functools.partial(kernel, scale, depth_total * scale), out...  80.1 us

profile of v5, /device:TPU:1, one launch (start us, length us, event | category | flops | bytes accessed | tf_op | source)
XLA Modules:
  0.0 82.9 jit_solution(194198662527779083)
XLA Ops:
  0.6 0.9 %copy.13 = bf16[2,2,96,128]{3,2,1,0:T(8,128)(2,1)S(1)} copy(bf16[2,2,96,128]{3,1,0,2:T(2,128)(2,1)} %bitcast.15) | data formatting | bytes 196608 | tf_op jit(solution)/shard_map/transpose | solution.py:712
  1.5 80.1 %shard_map.122 = (f32[3,2,972]{2,1,0:T(2,128)S(1)}, f32[3,2,3]{2,1,0:T(2,128)S(1)}) custom-call(bf16[4,96,128]{2,1,0:T(8,128)(2,1)S(1)} %bitcast.10, bf16[27,96,96]{2,1,0:T(8,128)(2,1)} %bitcast.13, bf16[27,96,96]{2,1,0:T(8,128)(2,1)} %bitcast.14, bf16[2,96]{1,0:T(2,128)(2,1)} %bitcast.17, bf16[4,96]{1,0:T(4,128)(2,1)} %bitcast.16, bf16[1,96]{1,0:T(2,128)(2,1)} %bitcast.18, ...), custom_call_target="tpu_custom_call" | custom-call | tf_op jit(solution)/shard_map/pallas_call | solution.py:763
  81.7 0.6 copy.16
  82.3 0.6 copy.17
